TPU v7x, 768 devices: a whole 4x8x12 slice. The times are simulated.
768 devices in a mesh: row: 8 (over x, core), col: 8 (over y), basis: 12 (over z).
Axes of the slice: x: 4, y: 8, z: 12, core: 2. Of those that a mesh axis runs over, the one named last changes fastest.
Arguments:
- block_data: bfloat16 [6144, 128, 128], P(('row', 'col', 'basis')), may hold values from -1.1953125 to 1.1953125
- item_pairs: int32 [6144, 2], P(('row', 'col', 'basis')), may hold values from 0 to 1023
- dest_slot: int32 [6144], P(('row', 'col', 'basis')), may hold values from 0 to 63, as said below
- brick_tag: int32 [6144], P(('row', 'col', 'basis')), may hold values from 0 to 23
- centres: float32 [1024, 3, 128], replicated, may hold values from -1.5 to 1.5
- exponents: float32 [1024, 128], replicated, may hold values from 4 to 12
- levels: int32 [1536], replicated, may hold values 0 or 1
- cell_pos: int32 [1536, 256], P(('row', 'col', 'basis')), may hold values from 0 to 4095, as said below
- corner_refs: int32 [1536, 256, 8], P(('row', 'col', 'basis')), may hold values from 0 to 12287, as said below
Outputs:
- density: float32 [1536, 4096], P(('row', 'col', 'basis'))
Inputs may be any that keep to these rules, and one draw needn't show every extreme that they name: `dest_slot`: on the rows of one device the values are distinct; value v sends the row to brick group v. `cell_pos`: within one brick the cells are distinct, one in each run of 16 consecutive points. `corner_refs`: index v names corner v % 8 of brick v // 8; every index occurs 256 times.
All inputs are finite; a program needn't handle non-finite values.
Results may differ from a plain program's by a relative error of at most 0.0028.
Values sent between devices are 32-bit elements; how exact they have to be, the bound alone decides.
A program may use at most 32 MiB of HBM per device.

v0:
```python
import jax
import jax.numpy as jnp
from jax import lax
from jax.sharding import PartitionSpec as P

EDGE = 16


coarse_spacing = 0.2


def basis_values(centres, exponents, block_index, level_value, edge_points):
    spacing = coarse_spacing * jnp.exp2(-level_value.astype(jnp.float32))
    coords = (jnp.arange(edge_points, dtype=jnp.float32) - (edge_points - 1) / 2.0) * spacing
    middle = centres[block_index]
    decay_rates = exponents[block_index]
    factor = jnp.exp(
        -decay_rates[None, :, None] * (coords[None, None, :] - middle[:, :, None]) ** 2
    )
    values_grid = (
        factor[0][:, :, None, None] * factor[1][:, None, :, None] * factor[2][:, None, None, :]
    )
    return values_grid.reshape(decay_rates.shape[0], edge_points * edge_points * edge_points)


def pair_density(block_values, pair_index, level_value, centres, exponents, edge_points):
    row_values = basis_values(centres, exponents, pair_index[0], level_value, edge_points)
    col_values = basis_values(centres, exponents, pair_index[1], level_value, edge_points).astype(
        jnp.bfloat16
    )
    product = jnp.dot(block_values, col_values, preferred_element_type=jnp.float32)
    return jnp.sum(row_values * product, axis=0)


def corner_points(edge_points):
    corner_code = jnp.arange(8, dtype=jnp.int32)
    first = corner_code // 4 * (edge_points - 1)
    second = corner_code // 2 % 2 * (edge_points - 1)
    third = corner_code % 2 * (edge_points - 1)
    return (first * edge_points + second) * edge_points + third


def body(
    block_data, item_pairs, dest_slot, brick_tag, centres, exponents, levels, cell_pos, corner_refs
):
    row_count = lax.axis_size("row")
    col_count = lax.axis_size("col")
    group_count = row_count * col_count
    item_count = block_data.shape[0]
    slot_depth = max(1, item_count // group_count)
    slot_count = group_count * slot_depth
    bricks_group = levels.shape[0] // group_count
    point_count = EDGE * EDGE * EDGE
    target = dest_slot // slot_depth * bricks_group + brick_tag
    item_level = levels[target]

    def single(operands):
        return pair_density(operands[0], operands[1], operands[2], centres, exponents, EDGE)

    densities = lax.map(single, (block_data, item_pairs, item_level))
    outgoing = jnp.zeros((slot_count, point_count), jnp.float32).at[dest_slot].set(densities)
    slot_tags = (
        jnp.zeros((slot_count,), jnp.float32).at[dest_slot].set(brick_tag.astype(jnp.float32))
    )
    arrived, arrived_tags = (
        lax.all_to_all(outgoing, ("row", "col"), split_axis=0, concat_axis=0, tiled=True),
        lax.all_to_all(slot_tags, ("row", "col"), split_axis=0, concat_axis=0, tiled=True),
    )
    selector = (
        arrived_tags[None, :] == jnp.arange(bricks_group, dtype=jnp.float32)[:, None]
    ).astype(jnp.float32)
    partial_sum = jnp.dot(selector, arrived, precision=lax.Precision.HIGHEST)
    own_density = lax.psum_scatter(partial_sum, "basis", scatter_dimension=0, tiled=True)
    corner_values = own_density[:, corner_points(EDGE)]
    all_corners = lax.all_gather(
        corner_values, ("row", "col", "basis"), axis=0, tiled=True
    ).reshape(-1)
    corner_mean = jnp.mean(all_corners[corner_refs], axis=-1)
    current = jnp.take_along_axis(own_density, cell_pos, axis=1)
    brick_rows = jnp.arange(own_density.shape[0], dtype=jnp.int32)[:, None]
    return own_density.at[brick_rows, cell_pos].set(0.5 * current + 0.5 * corner_mean)


def solution(mesh):
    return jax.shard_map(
        body,
        mesh=mesh,
        in_specs=(
            P(("row", "col", "basis"), None, None),
            P(("row", "col", "basis"), None),
            P(("row", "col", "basis")),
            P(("row", "col", "basis")),
            P(),
            P(),
            P(),
            P(("row", "col", "basis"), None),
            P(("row", "col", "basis"), None, None),
        ),
        out_specs=P(("row", "col", "basis"), None),
        check_vma=False,
    )
```

profile of v0, /device:TPU:1, one launch (start us, length us, event | category | flops | bytes accessed | tf_op | source)
XLA Modules:
  0.0 478.6 jit_solution(4415450004940134017)
XLA Ops:
  6.5 0.7 fusion.32
  8.6 14.6 %all-to-all-start = ((f32[64,1,1]{2,1,0:T(1,128)}), f32[64,1,1]{2,1,0:T(1,128)S(1)}, u32[]{:S(2)}, u32[]{:S(2)}) async-start(f32[64,1,1]{2,1,0:T(1,128)} %copy.25), calls=%async_computation | async-start | bytes 65536 | tf_op jit(solution)/shard_map/all_to_all | solution.py:67
  23.2 3.8 copy.26
  27.7 97.7 %while.12 = (s32[]{:T(128)}, f32[8,4096]{1,0:T(8,128)S(1)}, s32[8,2]{0,1:T(2,128)S(1)}, f32[1024,128]{1,0:T(8,128)}, s32[8]{0:T(128)S(1)}, /*index=5*/f32[1024,3...) while((s32[]{:T(128)}, f32[8,4096]{1,0:T(8,128)S(1)}, ...), condition=%wide.region_3.4_spmd, body=%wide.region_1.3_spmd.sunk | while | flops 136937776 | bytes 11301809 | solution.py:60
  31.9 0.7 fusion.42
  34.5 1.5 broadcast_multiply_fusion.7
  36.1 1.9 copy.39
  38.3 1.2 fusion.43
  44.1 0.7 fusion.42
  46.8 1.5 broadcast_multiply_fusion.7
  48.3 1.9 copy.39
  50.5 1.2 fusion.43
  56.3 0.7 fusion.42
  59.0 1.5 broadcast_multiply_fusion.7
  60.5 1.9 copy.39
  62.7 1.2 fusion.43
  68.5 0.7 fusion.42
  71.2 1.5 broadcast_multiply_fusion.7
  72.7 1.9 copy.39
  74.9 1.2 fusion.43
  80.7 0.7 fusion.42
  83.4 1.5 broadcast_multiply_fusion.7
  85.0 1.9 copy.39
  87.2 1.2 fusion.43
  93.0 0.7 fusion.42
  95.6 1.5 broadcast_multiply_fusion.7
  97.2 1.9 copy.39
  99.4 1.2 fusion.43
  105.2 0.7 fusion.42
  107.9 1.5 broadcast_multiply_fusion.7
  109.4 1.9 copy.39
  111.6 1.2 fusion.43
  120.1 1.5 broadcast_multiply_fusion.7
  121.6 1.9 copy.39
  123.8 1.2 fusion.43
  125.4 0.9 scatter_custom_fusion.1
  126.4 2.2 all_to_all.16
  128.5 10.3 %all-to-all-start.1 = ((f32[64,1,4096]{2,1,0:T(1,128)}), f32[64,1,4096]{2,1,0:T(1,128)S(1)}, u32[]{:S(2)}, u32[]{:S(2)}) async-start(f32[64,1,4096]{2,1,0:T(1,128)} %all_to_all.16), calls=%async_computation.1 | async-start | bytes 2097152 | tf_op jit(solution)/shard_map/all_to_all | solution.py:66
  139.3 1.3 dynamic-slice
  141.8 25.2 %all-to-all-done.1 = f32[64,1,4096]{2,1,0:T(1,128)S(1)} async-done(((f32[64,1,4096]{2,1,0:T(1,128)}), f32[64,1,4096]{2,1,0:T(1,128)S(1)}, u32[]{:S(2)}, u32[]{:S(2)}) %all-to-all-start.1) | async-done | bytes 1048608 | tf_op jit(solution)/shard_map/all_to_all | solution.py:66
  167.0 1.8 fusion.8
  168.8 104.9 %all-reduce.3.cloned.1.call-done = f32[24,4096]{1,0:T(8,128)} async-done(((f32[24,4096]{1,0:T(8,128)}), f32[24,4096]{1,0:T(8,128)}) %all-reduce.3.cloned.1.call-update) | async-done | bytes 393232
  273.7 0.9 constant_dynamic-slice_fusion.3
  275.3 4.8 %gather_fusion.3 = f32[512]{0:T(512)S(1)} fusion(f32[2,4096]{1,0:T(2,128)S(1)} %constant_dynamic-slice_fusion.3, s32[512]{0:T(512)S(1)} %bitcast.84), kind=kCustom, calls=%fused_computation.3 | custom fusion | bytes 8192 | tf_op jit(solution)/shard_map/jit(take_along_axis)/gather | solution.py:79
  280.8 99.8 %all-gather.1 = f32[768,2,8]{2,1,0:T(2,128)S(1)} all-gather(f32[1,2,8]{2,1,0:T(2,128)S(1)} %bitcast.88), channel_id=2, replica_groups=mesh['row'=8,'col'=8,'basis'=12] {'row','col','basis'}, dimensions={0}, use_global_device_ids=true | all-gather | bytes 49216 | tf_op jit(solution)/shard_map/all_gather | solution.py:75
  380.6 1.1 reshape.245
  381.7 23.0 %gather_fusion.2 = f32[4096]{0:T(1024)S(1)} fusion(f32[12288]{0:T(1024)S(1)} %reshape.245, s32[4096]{0:T(1024)S(1)} %broadcast_clamp_fusion), kind=kCustom, calls=%fused_computation.2 | custom fusion | bytes 49152 | tf_op jit(solution)/shard_map/gather | solution.py:78
  405.1 66.7 %scatter_fusion = f32[2,4096]{1,0:T(2,128)} fusion(f32[2,4096]{1,0:T(2,128)} %copy-done.1, s32[512]{0:T(512)S(1)} %bitcast.83, f32[512]{0:T(512)S(1)} %bitcast.86), kind=kCustom, calls=%fused_computation.6 | custom fusion | bytes 10240 | tf_op jit(solution)/shard_map/scatter | solution.py:81
  (125 shorter events, 26.5 us)
Async XLA Ops:
  6.5 20.5 %copy-start = (s32[1536]{0:T(1024)S(1)}, s32[1536]{0:T(1024)}, u32[]{:S(2)}) copy-start(s32[1536]{0:T(1024)} %param.17) | copy-start | bytes 18436
  8.6 120.0 %all-to-all-start = ((f32[64,1,1]{2,1,0:T(1,128)}), f32[64,1,1]{2,1,0:T(1,128)S(1)}, u32[]{:S(2)}, u32[]{:S(2)}) async-start(f32[64,1,1]{2,1,0:T(1,128)} %copy.25), calls=%async_computation | async-start | bytes 65536 | tf_op jit(solution)/shard_map/all_to_all | solution.py:67
  23.2 4.5 copy-start.2
  126.4 12.6 %copy-start.4 = (s32[2,256]{1,0:T(2,128)S(1)}, s32[2,256]{1,0:T(2,128)}, u32[]{:S(2)}) copy-start(s32[2,256]{1,0:T(2,128)} %param.18) | copy-start | bytes 6148
  126.4 12.6 %copy-start.3 = (s32[2,256,8]{1,2,0:T(8,128)S(1)}, s32[2,256,8]{1,2,0:T(8,128)}, u32[]{:S(2)}) copy-start(s32[2,256,8]{1,2,0:T(8,128)} %param.19) | copy-start | bytes 49156
  128.5 38.4 %all-to-all-start.1 = ((f32[64,1,4096]{2,1,0:T(1,128)}), f32[64,1,4096]{2,1,0:T(1,128)S(1)}, u32[]{:S(2)}, u32[]{:S(2)}) async-start(f32[64,1,4096]{2,1,0:T(1,128)} %all_to_all.16), calls=%async_computation.1 | async-start | bytes 2097152 | tf_op jit(solution)/shard_map/all_to_all | solution.py:66
  138.9 134.8 %all-reduce.3.cloned.1.call-start = ((), (), s32[]{:S(2)}) async-start(), calls=%async_computation.2 | async-start | bytes 786432
  274.6 5.5 %copy-start.1 = (f32[2,4096]{1,0:T(2,128)}, f32[2,4096]{1,0:T(2,128)S(1)}, u32[]{:S(2)}) copy-start(f32[2,4096]{1,0:T(2,128)S(1)} %constant_dynamic-slice_fusion.3) | copy-start | bytes 98308
Sparse Core Ops, SparseCore 0:
  168.9 104.7 all-reduce.2
where the time goes:
time: 486 us; the launch traced here: 479 us
  local copies, waits for them, and re-layouts  142 us (29%)
  waiting for transfers between devices  130 us (27%)
  blocking collectives  99.8 us (21%)
  loops' own time  33.4 us (7%)
  starting transfers between devices  25 us (5%)
  other arithmetic  22.4 us (5%)
  between operations  14.3 us (3%)
  matrix products  11.6 us (2%)
    unnamed x2, waiting for transfers between devices  105 us
    all_gather x1, blocking collectives, body(): lax.all_gather(corner_values, ('row', 'col', 'basis'), axis=0, tiled=True)  99.8 us
    scatter x1, local copies, waits for them, and re-layouts, body(): own_density.at[brick_rows, cell_pos].set(0.5 * current + 0.5 * corner_mean)  66.7 us
    another operation x1, loops' own time, body(): densities = lax.map(single, (block_data, item_pairs, item_level))  33.4 us
    all_to_all x1, waiting for transfers between devices, body(): lax.all_to_all(outgoing, ('row', 'col'), split_axis=0, concat_axis=0, til...  25.2 us
    gather x2, local copies, waits for them, and re-layouts, body(): corner_mean = jnp.mean(all_corners[corner_refs], axis=-1)  23.2 us
    mul x16, local copies, waits for them, and re-layouts, basis_values(): factor[0][:, :, None, None] * factor[1][:, None, :, None]  15.4 us
    all_to_all x1, starting transfers between devices, body(): lax.all_to_all(slot_tags, ('row', 'col'), split_axis=0, concat_axis=0, ti...  14.6 us
  transfers between devices with their start and end apart: 3, of which 2 were waited for; matrix products, arithmetic and copies ran while one was open for 15% of the time, Pallas kernels for 0%

commit v1 on v0

v1 whole, which is shorter than its diff:
```python
import jax
import jax.numpy as jnp
from jax import lax
from jax.experimental import pallas as pl
from jax.experimental.pallas import tpu as pltpu
from jax.sharding import PartitionSpec as P

MESH = pl.DeviceIdType.MESH
F32 = jnp.float32
BF16 = jnp.bfloat16

EDGE = 16
HALF = (EDGE - 1) / 2.0
PTS = EDGE**3
BS = 128
ITEMS = 8
NR, NC, NZ = 8, 8, 12
GROUP = 24
SUB = 43
CHUNK = SUB * NC
WIDE = 384
ROWS = 48
NT = (((1,), (1,)), ((), ()))
CORNERS = tuple(
    ((c // 4) * 15 * EDGE + (c // 2 % 2) * 15) * EDGE + (c % 2) * 15 for c in range(8)
)


def lanes(shape):
    return lax.broadcasted_iota(jnp.int32, shape, len(shape) - 1)


def rows(shape):
    return lax.broadcasted_iota(jnp.int32, shape, len(shape) - 2)


def roll(x, shift):
    shift %= x.shape[-1]
    return x if shift == 0 else pltpu.roll(x, shift, x.ndim - 1)


def density_kernel(
    pairs_ref, slot_ref, tag_ref, levels_ref, cen_ref, exp_ref, block_ref, out_ref, dens_ref
):
    step16 = rows((EDGE, BS)).astype(F32) - HALF
    lane256 = lanes((1, EDGE * EDGE))
    step_y = (lane256 // EDGE).astype(F32) - HALF
    step_z = (lane256 % EDGE).astype(F32) - HALF
    step_x = lanes((1, BS)).astype(F32) - HALF
    dens_ref[:, PTS:] = jnp.zeros((ITEMS, dens_ref.shape[1] - PTS), F32)

    def item(k, targets):
        first, second = pairs_ref[0, k], pairs_ref[1, k]
        target = slot_ref[k] * GROUP + tag_ref[k]
        spacing = jnp.where(levels_ref[target] == 0, 0.2, 0.1).astype(F32)

        rate = exp_ref[pl.ds(second, 1), :]
        middle = [cen_ref[d, pl.ds(second, 1), :] for d in range(3)]
        col_x, col_y, col_z = [jnp.exp(-rate * (step16 * spacing - m) ** 2) for m in middle]
        col_yz = jnp.concatenate([col_y[y : y + 1] * col_z for y in range(EDGE)], axis=0)

        params = jnp.concatenate(
            [exp_ref[pl.ds(first, 1), :]]
            + [cen_ref[d, pl.ds(first, 1), :] for d in range(3)]
            + [jnp.zeros((4, BS), F32)],
            axis=0,
        )
        columns = jnp.transpose(params)
        decay = -columns[:, 0:1]
        row_x = jnp.exp(decay * (step_x * spacing - columns[:, 1:2]) ** 2)
        row_yz = jnp.exp(
            decay
            * (
                (step_y * spacing - columns[:, 2:3]) ** 2
                + (step_z * spacing - columns[:, 3:4]) ** 2
            )
        )
        block = block_ref[k]
        for x in range(EDGE):
            col_values = (col_x[x : x + 1] * col_yz).astype(BF16)
            product = lax.dot_general(block, col_values, NT, preferred_element_type=F32)
            weighted = product * row_yz * row_x[:, x : x + 1]
            dens_ref[pl.ds(k, 1), x * 256 : x * 256 + 256] = jnp.sum(
                weighted, axis=0, keepdims=True
            )
        return jnp.where(rows((ITEMS, BS)) == k, target.astype(F32), targets)

    targets = lax.fori_loop(0, ITEMS, item, jnp.zeros((ITEMS, BS), F32))

    lane = lanes((ITEMS, 128))
    base = CHUNK % 128
    extra = jnp.where(lane == base + 8, targets, 0.0)
    for c, q in enumerate(CORNERS):
        tile = dens_ref[:, q // 128 * 128 : q // 128 * 128 + 128]
        extra = jnp.where(lane == base + c, roll(tile, base + c - q), extra)
    for z in range(NZ):
        for j in range(WIDE // 128):
            start = z * CHUNK + j * 128
            tile, shift = start // 128, start % 128
            value = roll(dens_ref[:, tile * 128 : tile * 128 + 128], -shift)
            if shift:
                after = roll(dens_ref[:, tile * 128 + 128 : tile * 128 + 256], -shift)
                value = jnp.where(lane < 128 - shift, value, after)
            if j == CHUNK // 128:
                value = jnp.where(lane < base, value, extra)
            out_ref[z, :, j * 128 : j * 128 + 128] = value


def exchange_kernel(
    zs_ref,
    own_ref,
    tab_ref,
    z_got,
    turned,
    y_out,
    y_got,
    r_out,
    r_got,
    b_out,
    b_got,
    f_out,
    f_got,
    c_out,
    c_got,
    send_sem,
    recv_sem,
):
    me = {a: lax.axis_index(a) for a in ("row", "col", "basis")}
    size = {"row": NR, "col": NC, "basis": NZ}

    def device(axis, index):
        return tuple(index if a == axis else me[a] for a in ("row", "col", "basis"))

    barrier = pltpu.get_barrier_semaphore()
    for axis in ("basis", "col", "row"):
        for k in range(1, size[axis]):
            pl.semaphore_signal(
                barrier,
                inc=1,
                device_id=device(axis, lax.rem(me[axis] + k, size[axis])),
                device_id_type=MESH,
            )
    pl.semaphore_wait(barrier, NR + NC + NZ - 3)

    def start(axis, out, got, stage, each):
        copies = []
        for k in range(1, size[axis]):
            to = lax.rem(me[axis] + k, size[axis])
            copy = pltpu.make_async_remote_copy(
                src_ref=out.at[to] if each else out,
                dst_ref=got.at[me[axis]],
                send_sem=send_sem.at[stage, k],
                recv_sem=recv_sem.at[stage, k],
                device_id=device(axis, to),
                device_id_type=MESH,
            )
            copy.start()
            copies.append(copy)
        got[me[axis]] = out[me[axis]] if each else out[...]
        return copies

    def arrive(copies):
        for copy in copies:
            copy.wait_recv()

    lane = lanes((24, 128))

    z_copies = start("basis", zs_ref, z_got, 0, True)
    arrive(z_copies)
    held = jnp.concatenate(
        [z_got[...].reshape(NZ * ITEMS, WIDE), jnp.zeros((128 - NZ * ITEMS, WIDE), F32)], axis=0
    )
    turned[...] = jnp.transpose(held)

    row = rows((ROWS, 128))
    for y in range(NC):
        slab = turned[y * SUB : y * SUB + ROWS, :]
        corner = turned[CHUNK + y : CHUNK + y + 1, :]
        target = turned[CHUNK + 8 : CHUNK + 9, :]
        y_out[y] = jnp.where(row < SUB, slab, jnp.where(row == SUB, corner, target))
    y_copies = start("col", y_out, y_got, 1, True)
    arrive(y_copies)

    pieces = []
    targets = []
    for y in range(NC):
        value = y_got[y]
        high = value.astype(BF16)
        low = (value - high.astype(F32)).astype(BF16)
        pieces.append(jnp.concatenate([high, low], axis=0))
        targets.append(y_got[y, SUB + 1 : SUB + 2, :])
    left = jnp.concatenate(pieces, axis=1)
    brick = rows((128, 128)).astype(F32)

    def table(base, upper):
        number = brick + float(base)
        if upper:
            number = number + jnp.where(brick >= 64.0, float(upper), 0.0)
        right = jnp.concatenate(
            [jnp.where(number == t, 1.0, 0.0).astype(BF16) for t in targets], axis=1
        )
        both = lax.dot_general(left, right, NT, preferred_element_type=F32)
        return both[:ROWS] + both[ROWS:]

    for j in range(NR // 2):
        r_out[2 * j, :ROWS] = table(384 * j, 0)
        r_out[2 * j + 1, :ROWS] = table(384 * j + 192, 0)
        mixed = table(384 * j + 128, 128)
        upper, lower = mixed[:24], mixed[24:]
        r_out[2 * j, ROWS:] = jnp.where(lane < 64, upper, roll(lower, 64))
        r_out[2 * j + 1, ROWS:] = jnp.where(lane < 64, roll(upper, 64), lower)

    r_copies = start("row", r_out, r_got, 2, True)
    arrive(r_copies)
    total = r_got[0]
    for r in range(1, NR):
        total = total + r_got[r]
    head, tail = total[:ROWS], total[ROWS:]
    tail = jnp.concatenate([tail, roll(tail, 64)], axis=0)
    both = jnp.concatenate([head, tail], axis=1)
    bricks = jnp.transpose(jnp.concatenate([both, jnp.zeros((128 - ROWS, 256), F32)], axis=0))

    corner_rows = jnp.concatenate(
        [head[SUB : SUB + 1], tail[SUB : SUB + 1], jnp.zeros((6, 128), F32)], axis=0
    )
    for y in range(NC):
        b_out[y, :GROUP] = bricks[y * GROUP : y * GROUP + GROUP]
        b_out[y, GROUP:] = corner_rows
    b_copies = start("col", b_out, b_got, 3, True)
    arrive(b_copies)

    for y in range(NC):
        c_out[y : y + 1, :128] = b_got[y, GROUP : GROUP + 1, :]
        c_out[y : y + 1, 128:] = b_got[y, GROUP + 1 : GROUP + 2, :]
    c_copies = start("row", c_out, c_got, 4, False)

    for j in range(WIDE // 128):
        value = jnp.zeros((GROUP, 128), F32)
        for y in range(NC):
            first, last = y * SUB - j * 128, (y + 1) * SUB - j * 128
            if first < 128 and last > 0:
                moved = roll(b_got[y, :GROUP], first)
                value = jnp.where((lane >= first) & (lane < last), moved, value)
        for z in range(NZ):
            f_out[z, :, j * 128 : j * 128 + 128] = value[2 * z : 2 * z + 2]
    f_copies = start("basis", f_out, f_got, 5, True)
    arrive(f_copies)
    lane2 = lanes((2, 128))
    for t in range(PTS // 128):
        value = None
        for z in range(NZ):
            first, last = z * CHUNK - t * 128, (z + 1) * CHUNK - t * 128
            if first < 128 and last > 0:
                tile, shift = (-first) // 128, (-first) % 128
                part = None
                for at in (tile, tile + 1):
                    low = at * 128 + first
                    if 0 <= at < WIDE // 128 and low < 128 and low + 128 > 0:
                        moved = roll(f_got[z, :, at * 128 : at * 128 + 128], low)
                        part = moved if part is None else jnp.where(lane2 < low, part, moved)
                value = part if value is None else jnp.where(lane2 < first, value, part)
        own_ref[:, t * 128 : t * 128 + 128] = value
    arrive(c_copies)
    tab_ref[...] = c_got[...]
    for copies in (z_copies, y_copies, r_copies, b_copies, c_copies, f_copies):
        for copy in copies:
            copy.wait_send()


def finish_kernel(own_ref, tab_ref, refs_ref, cell_ref, out_ref):
    for b in range(2):
        means = []
        for h in range(2):
            ref = refs_ref[b, :, h * 128 : h * 128 + 128]
            corner, brick = ref & 7, ref >> 3
            source = ((brick >> 6) * 11) >> 5
            place = brick - source * 192
            at = place & 127
            which = (source * 2 + (place >> 7)) * 8 + corner
            found = jnp.zeros((8, 128), F32)
            for r in range(NR):
                for half in range(2):
                    for c in range(8):
                        line = jnp.broadcast_to(
                            tab_ref[r, c : c + 1, half * 128 : half * 128 + 128], (8, 128)
                        )
                        here = jnp.take_along_axis(line, at, axis=1)
                        found = jnp.where(which == (r * 2 + half) * 8 + c, here, found)
            means.append(jnp.sum(found, axis=0, keepdims=True) * 0.0625)
        mean = jnp.concatenate(means, axis=1)
        cell = cell_ref[b : b + 1, :]
        upper = rows((32, 256)) == (cell >> 7)
        high = mean.astype(BF16).astype(F32)
        left = jnp.concatenate(
            [
                jnp.where(upper, high, 0.0),
                jnp.where(upper, mean - high, 0.0),
                jnp.where(upper, 0.5, 0.0),
            ],
            axis=0,
        ).astype(BF16)
        right = jnp.where(rows((128, 256)) == (cell & 127), 1.0, 0.0).astype(BF16)
        spread = lax.dot_general(left, right, NT, preferred_element_type=F32)
        added, kept = spread[:32] + spread[32:64], 1.0 - spread[64:]
        for t in range(PTS // 128):
            part = slice(t * 128, t * 128 + 128)
            out_ref[b : b + 1, part] = (
                own_ref[b : b + 1, part] * kept[t : t + 1] + added[t : t + 1]
            )


def body(
    block_data, item_pairs, dest_slot, brick_tag, centres, exponents, levels, cell_pos, corner_refs
):
    vmem = pl.BlockSpec(memory_space=pltpu.VMEM)
    smem = pl.BlockSpec(memory_space=pltpu.SMEM)
    chunks = pl.pallas_call(
        density_kernel,
        out_shape=jax.ShapeDtypeStruct((NZ, ITEMS, WIDE), F32),
        in_specs=[smem] * 4 + [vmem] * 3,
        out_specs=vmem,
        scratch_shapes=[pltpu.VMEM((ITEMS, 34 * 128), F32)],
        compiler_params=pltpu.CompilerParams(vmem_limit_bytes=32 * 2**20),
        name="pair_density",
    )(
        item_pairs.T,
        dest_slot,
        brick_tag,
        levels,
        centres.transpose(1, 0, 2),
        exponents,
        block_data,
    )
    own, corners = pl.pallas_call(
        exchange_kernel,
        out_shape=(
            jax.ShapeDtypeStruct((2, PTS), F32),
            jax.ShapeDtypeStruct((NR, 8, 256), F32),
        ),
        in_specs=[vmem],
        out_specs=(vmem, vmem),
        scratch_shapes=[
            pltpu.VMEM((NZ, ITEMS, WIDE), F32),
            pltpu.VMEM((WIDE, 128), F32),
            pltpu.VMEM((NC, ROWS, 128), F32),
            pltpu.VMEM((NC, ROWS, 128), F32),
            pltpu.VMEM((NR, ROWS + 24, 128), F32),
            pltpu.VMEM((NR, ROWS + 24, 128), F32),
            pltpu.VMEM((NC, GROUP + 8, 128), F32),
            pltpu.VMEM((NC, GROUP + 8, 128), F32),
            pltpu.VMEM((NZ, 2, WIDE), F32),
            pltpu.VMEM((NZ, 2, WIDE), F32),
            pltpu.VMEM((8, 256), F32),
            pltpu.VMEM((NR, 8, 256), F32),
            pltpu.SemaphoreType.DMA((6, NZ)),
            pltpu.SemaphoreType.DMA((6, NZ)),
        ],
        compiler_params=pltpu.CompilerParams(
            collective_id=0, has_side_effects=True, vmem_limit_bytes=32 * 2**20
        ),
        name="exchange",
    )(chunks)
    return pl.pallas_call(
        finish_kernel,
        out_shape=jax.ShapeDtypeStruct((2, PTS), F32),
        in_specs=[vmem] * 4,
        out_specs=vmem,
        compiler_params=pltpu.CompilerParams(vmem_limit_bytes=32 * 2**20),
        name="cells",
    )(own, corners, corner_refs.transpose(0, 2, 1), cell_pos)


def solution(mesh):
    spread = ("row", "col", "basis")
    return jax.shard_map(
        body,
        mesh=mesh,
        in_specs=(
            P(spread, None, None),
            P(spread, None),
            P(spread),
            P(spread),
            P(),
            P(),
            P(),
            P(spread, None),
            P(spread, None, None),
        ),
        out_specs=P(spread, None),
        check_vma=False,
    )
```

time: 486 us -> 68.2 us (0.14); the launches traced: 479 us -> 67.9 us
  local copies, waits for them, and re-layouts: 142 us -> 6.1 us
  waiting for transfers between devices: 130 us -> 0 us
  blocking collectives: 99.8 us -> 0 us
  Pallas kernels: 0 us -> 61.8 us
  loops' own time: 33.4 us -> 0 us
  starting transfers between devices: 25 us -> 0 us
  other arithmetic: 22.4 us -> 0 us
  between operations: 14.3 us -> 0.04 us
  matrix products: 11.6 us -> 0 us
    unnamed x2 -> x0, waiting for transfers between devices: 105 us -> none
    all_gather x1 -> x0, blocking collectives: 99.8 us -> none  [body(): lax.all_gather(corner_values, ('row', 'col', 'basis'), axis=0, tiled=True)]
    scatter x3 -> x0, local copies, waits for them, and re-layouts: 68.2 us -> none  [the longest x1 66.7 us: body(): own_density.at[brick_rows, cell_pos].set(0.5 * current + 0.5 * corner_mean)]
    pallas_call x0 -> x3, Pallas kernels: none -> 61.8 us  [the longest x1 54.2 us: body(): pl.pallas_call(exchange_kernel, out_shape=(jax.ShapeDtypeStruct((2, PTS),...]
    another operation x1 -> x0, loops' own time: 33.4 us -> none  [body(): densities = lax.map(single, (block_data, item_pairs, item_level))]
    gather x7 -> x0, local copies, waits for them, and re-layouts: 29.3 us -> none  [the longest x2 23.2 us: body(): corner_mean = jnp.mean(all_corners[corner_refs], axis=-1)]
    all_to_all x2 -> x0, waiting for transfers between devices: 25.2 us -> none  [the longest x1 25.2 us: body(): lax.all_to_all(outgoing, ('row', 'col'), split_axis=0, concat_axis=0, til...]
    all_to_all x2 -> x0, starting transfers between devices: 24.9 us -> none  [the longest x1 14.6 us: body(): lax.all_to_all(slot_tags, ('row', 'col'), split_axis=0, concat_axis=0, ti...]
  transfers between devices with their start and end apart: 3 -> 0, of which waited for: 2 -> 0; matrix products, arithmetic and copies ran while one was open for 15% -> 0% of each run, Pallas kernels for 0% -> 0%
where the time goes in v1:
time: 68.2 us; the launch traced here: 67.9 us
  Pallas kernels  61.8 us (91%)
  local copies, waits for them, and re-layouts  6.1 us (9%)
    pallas_call x1, Pallas kernels, body(): pl.pallas_call(exchange_kernel, out_shape=(jax.ShapeDtypeStruct((2, PTS),...  54.2 us
    pallas_call x1, Pallas kernels, body(): pl.pallas_call(density_kernel, out_shape=jax.ShapeDtypeStruct((NZ, ITEMS,...  6.2 us
    unnamed x18, local copies, waits for them, and re-layouts  6.1 us
    pallas_call x1, Pallas kernels, body(): pl.pallas_call(finish_kernel, out_shape=jax.ShapeDtypeStruct((2, PTS), F3...  1.41 us

profile of v1, /device:TPU:1, one launch (start us, length us, event | category | flops | bytes accessed | tf_op | source)
XLA Modules:
  0.0 67.9 jit_solution(6971471099205040253)
XLA Ops:
  0.0 0.0 copy-start.5
  0.0 0.0 copy-start
  0.0 1.4 %copy-done = f32[1024,3,128]{2,0,1:T(8,128)S(1)} copy-done((f32[1024,3,128]{2,0,1:T(8,128)S(1)}, f32[1024,3,128]{2,0,1:T(8,128)}, u32[]{:S(2)}) %copy-start) | copy-done | bytes 1572888
  1.4 0.0 copy-start.1
  1.4 1.0 %copy-done.1 = f32[1024,128]{1,0:T(8,128)S(1)} copy-done((f32[1024,128]{1,0:T(8,128)S(1)}, f32[1024,128]{1,0:T(8,128)}, u32[]{:S(2)}) %copy-start.1) | copy-done | bytes 524312
  2.5 0.0 copy-start.2
  2.5 0.9 %copy-done.2 = bf16[8,128,128]{2,1,0:T(8,128)(2,1)S(1)} copy-done((bf16[8,128,128]{2,1,0:T(8,128)(2,1)S(1)}, bf16[8,128,128]{2,1,0:T(8,128)(2,1)}, u32[]{:S(2)}) %copy-start.2) | copy-done | bytes 262168
  3.4 0.0 copy-start.4
  3.4 0.7 %copy-done.4 = s32[1536]{0:T(1024)S(1)} copy-done((s32[1536]{0:T(1024)S(1)}, s32[1536]{0:T(1024)}, u32[]{:S(2)}) %copy-start.4) | copy-done | bytes 6168
  4.1 0.0 copy-start.6
  4.1 0.7 copy-done.6
  4.8 0.0 copy-start.7
  4.8 0.7 copy-done.7
  5.5 0.0 copy-start.8
  5.5 0.7 copy-done.8
  6.1 0.0 copy-start.3
  6.1 6.2 %pair_density.1.zs_ref = f32[12,8,384]{2,1,0:T(8,128)S(1)} custom-call(s32[2,8]{1,0:T(2,128)S(1)} %bitcast.5, s32[8]{0:T(128)S(1)} %copy-done.7, s32[8]{0:T(128)S(1)} %copy-done.8, s32[1536]{0:T(1024)S(1)} %copy-done.4, f32[3,1024,128]{2,1,0:T(8,128)S(1)} %bitcast.3, f32[1024,128]{1,0:T(8,128)S(1)} %copy-done.1, bf16[8,128,128]{2,1,0:T(8,128)(2,1)S(1)} %copy-done.2), custom_call_target="tpu_custom_call" | custom-call | tf_op jit(solution)/shard_map/pair_density/pallas_call | solution.py:317
  12.3 54.2 %exchange.1 = (f32[2,4096]{1,0:T(2,128)S(1)}, f32[8,8,256]{2,1,0:T(8,128)S(1)}) custom-call(f32[12,8,384]{2,1,0:T(8,128)S(1)} %pair_density.1.zs_ref), custom_call_target="tpu_custom_call" | custom-call | tf_op jit(solution)/shard_map/exchange/pallas_call | solution.py:334
  66.5 0.0 copy-done.5
  66.5 0.0 copy-done.3
  66.5 1.4 %cells.1 = f32[2,4096]{1,0:T(2,128)} custom-call(f32[2,4096]{1,0:T(2,128)S(1)} %get-tuple-element.7.own_ref, f32[8,8,256]{2,1,0:T(8,128)S(1)} %get-tuple-element.8.tab_ref, s32[2,8,256]{2,1,0:T(8,128)S(1)} %bitcast.4, s32[2,256]{1,0:T(2,128)S(1)} %copy-done.5), custom_call_target="tpu_custom_call" | custom-call | tf_op jit(solution)/shard_map/cells/pallas_call | solution.py:363
Async XLA Ops:
  0.0 66.5 %copy-start.5 = (s32[2,256]{1,0:T(2,128)S(1)}, s32[2,256]{1,0:T(2,128)}, u32[]{:S(2)}) copy-start(s32[2,256]{1,0:T(2,128)} %cell_ref.1) | copy-start | bytes 6148
  0.0 1.4 %copy-start = (f32[1024,3,128]{2,0,1:T(8,128)S(1)}, f32[1024,3,128]{2,0,1:T(8,128)}, u32[]{:S(2)}) copy-start(f32[1024,3,128]{2,0,1:T(8,128)} %param.13) | copy-start | bytes 4718596
  1.4 1.0 %copy-start.1 = (f32[1024,128]{1,0:T(8,128)S(1)}, f32[1024,128]{1,0:T(8,128)}, u32[]{:S(2)}) copy-start(f32[1024,128]{1,0:T(8,128)} %exp_ref.1) | copy-start | bytes 1572868
  2.5 0.9 %copy-start.2 = (bf16[8,128,128]{2,1,0:T(8,128)(2,1)S(1)}, bf16[8,128,128]{2,1,0:T(8,128)(2,1)}, u32[]{:S(2)}) copy-start(bf16[8,128,128]{2,1,0:T(8,128)(2,1)} %block_ref.1) | copy-start | bytes 786436
  3.4 0.7 %copy-start.4 = (s32[1536]{0:T(1024)S(1)}, s32[1536]{0:T(1024)}, u32[]{:S(2)}) copy-start(s32[1536]{0:T(1024)} %levels_ref.1) | copy-start | bytes 18436
  4.1 0.7 copy-start.6
  4.8 0.7 copy-start.7
  5.5 0.7 copy-start.8
  6.1 60.4 %copy-start.3 = (s32[2,256,8]{1,2,0:T(8,128)S(1)}, s32[2,256,8]{1,2,0:T(8,128)}, u32[]{:S(2)}) copy-start(s32[2,256,8]{1,2,0:T(8,128)} %param.17) | copy-start | bytes 49156

commit v2 on v0

v2 whole, which is shorter than its diff:
```python
import itertools

import jax
import jax.numpy as jnp
from jax import lax
from jax.experimental import pallas as pl
from jax.experimental.pallas import tpu as pltpu
from jax.sharding import PartitionSpec as P

MESH = pl.DeviceIdType.MESH
F32 = jnp.float32
BF16 = jnp.bfloat16

EDGE = 16
HALF = (EDGE - 1) / 2.0
PTS = EDGE**3
BS = 128
ITEMS = 8
NR, NC, NZ = 8, 8, 12
PLANE = NC * NZ
GROUP = 24
OWN = NC * GROUP
SUB = 43
TARGET = SUB
CORNER = 48
ROWS = 56
NT = (((1,), (1,)), ((), ()))
CORNERS = tuple(
    ((c // 4) * 15 * EDGE + (c // 2 % 2) * 15) * EDGE + (c % 2) * 15 for c in range(8)
)


def far(step, size):
    return min(step, size - step)


PLANE_STEPS = sorted(
    (s for s in itertools.product(range(NC), range(NZ)) if any(s)),
    key=lambda s: -(far(s[0], NC) + far(s[1], NZ)),
)
ROW_STEPS = ((2, 1), (2, 0), (1, 1), (3, 1), (1, 0), (3, 0), (0, 1))


def lanes(shape):
    return lax.broadcasted_iota(jnp.int32, shape, len(shape) - 1)


def rows(shape):
    return lax.broadcasted_iota(jnp.int32, shape, len(shape) - 2)


def roll(x, shift):
    shift %= x.shape[-1]
    return x if shift == 0 else pltpu.roll(x, shift, x.ndim - 1)


def kernel(
    pairs_hbm,
    slot_hbm,
    tag_hbm,
    levels_hbm,
    cen_hbm,
    exp_hbm,
    block_hbm,
    refs_hbm,
    cell_hbm,
    out_ref,
    pairs_ref,
    slot_ref,
    tag_ref,
    levels_ref,
    cen_ref,
    exp_ref,
    block_ref,
    refs_ref,
    cell_ref,
    dens_ref,
    a_out,
    a_got,
    r_out,
    r_got,
    b_out,
    b_got,
    c_out,
    c_got,
    load_sem,
    again_sem,
    a_send,
    a_recv,
    r_send,
    r_recv,
    b_send,
    b_recv,
    c_send,
    c_recv,
):
    loads = [
        pltpu.make_async_copy(source, into, load_sem.at[n])
        for n, (source, into) in enumerate(
            (
                (pairs_hbm, pairs_ref),
                (slot_hbm, slot_ref),
                (tag_hbm, tag_ref),
                (levels_hbm, levels_ref),
                (cen_hbm, cen_ref),
                (exp_hbm, exp_ref),
                (block_hbm, block_ref),
                (refs_hbm, refs_ref),
                (cell_hbm, cell_ref),
            )
        )
    ]
    for load in loads:
        load.start()

    r, y, z = (lax.axis_index(a) for a in ("row", "col", "basis"))
    ys = [lax.rem(y + n, NC) for n in range(NC)]
    zs = [lax.rem(z + n, NZ) for n in range(NZ)]
    x, core = r // 2, lax.rem(r, 2)
    xs = [lax.rem(x + n, NR // 2) * 2 for n in range(NR // 2)]
    cores = [core, 1 - core]
    row_of = [xs[dx] + cores[dc] for dx, dc in ROW_STEPS]
    me = y * NZ + z

    barrier = pltpu.get_barrier_semaphore()
    for n in range(1, NZ):
        pl.semaphore_signal(barrier, inc=1, device_id=(r, y, zs[n]), device_id_type=MESH)
    for n in range(1, NC):
        pl.semaphore_signal(barrier, inc=1, device_id=(r, ys[n], z), device_id_type=MESH)
    for other in row_of:
        pl.semaphore_signal(barrier, inc=1, device_id=(other, y, z), device_id_type=MESH)

    step16 = rows((EDGE, BS)).astype(F32) - HALF
    lane256 = lanes((1, EDGE * EDGE))
    step_y = (lane256 // EDGE).astype(F32) - HALF
    step_z = (lane256 % EDGE).astype(F32) - HALF
    step_x = lanes((1, BS)).astype(F32) - HALF
    dens_ref[:, PTS:] = jnp.zeros((ITEMS, dens_ref.shape[1] - PTS), F32)
    for load in loads:
        load.wait()

    def item(k, targets):
        first, second = pairs_ref[0, k], pairs_ref[1, k]
        group, tag = slot_ref[k], tag_ref[k]
        spacing = jnp.where(levels_ref[group * GROUP + tag] == 0, 0.2, 0.1).astype(F32)

        rate = exp_ref[pl.ds(second, 1), :]
        middle = [cen_ref[d, pl.ds(second, 1), :] for d in range(3)]
        col_x, col_y, col_z = [jnp.exp(-rate * (step16 * spacing - m) ** 2) for m in middle]
        col_yz = jnp.concatenate([col_y[n : n + 1] * col_z for n in range(EDGE)], axis=0)

        params = jnp.concatenate(
            [exp_ref[pl.ds(first, 1), :]]
            + [cen_ref[d, pl.ds(first, 1), :] for d in range(3)]
            + [jnp.zeros((4, BS), F32)],
            axis=0,
        )
        columns = jnp.transpose(params)
        decay = -columns[:, 0:1]
        row_x = jnp.exp(decay * (step_x * spacing - columns[:, 1:2]) ** 2)
        row_yz = jnp.exp(
            decay
            * (
                (step_y * spacing - columns[:, 2:3]) ** 2
                + (step_z * spacing - columns[:, 3:4]) ** 2
            )
        )
        block = block_ref[k]
        for n in range(EDGE):
            col_values = (col_x[n : n + 1] * col_yz).astype(BF16)
            product = lax.dot_general(block, col_values, NT, preferred_element_type=F32)
            weighted = product * row_yz * row_x[:, n : n + 1]
            dens_ref[pl.ds(k, 1), n * 256 : n * 256 + 256] = jnp.sum(
                weighted, axis=0, keepdims=True
            )
        place = (group & 7) * GROUP + tag
        number = (group >> 3) * OWN + (place & 1) * PLANE + (place >> 1)
        return jnp.where(rows((ITEMS, 128)) == k, number.astype(F32), targets)

    numbers = lax.fori_loop(0, ITEMS // 2, item, jnp.zeros((ITEMS, 128), F32))
    pl.semaphore_wait(barrier, NR + NC + NZ - 3)
    for n in range(1, NC):
        pl.semaphore_signal(again_sem, inc=1, device_id=(r, ys[n], z), device_id_type=MESH)
    numbers = lax.fori_loop(ITEMS // 2, ITEMS, item, numbers)

    lane = lanes((ITEMS, 128))
    extra = jnp.where(lane == TARGET, numbers, 0.0)
    for c, q in enumerate(CORNERS):
        tile = dens_ref[:, q // 128 * 128 : q // 128 * 128 + 128]
        extra = jnp.where(lane == CORNER + c, roll(tile, CORNER + c - q), extra)
    half = lanes((4, 128)) < 64
    for a in range(PLANE):
        tile, shift = a * SUB // 128, a * SUB % 128
        value = roll(dens_ref[:, tile * 128 : tile * 128 + 128], -shift)
        if shift + SUB > 128:
            after = roll(dens_ref[:, tile * 128 + 128 : tile * 128 + 256], -shift)
            value = jnp.where(lane < 128 - shift, value, after)
        value = jnp.where(lane < SUB, value, extra)
        a_out[a] = jnp.where(half, value[:4], roll(value, 64)[4:])
    pl.semaphore_wait(again_sem, NC - 1)

    def plane_copies(out, got, send, recv):
        return [
            pltpu.make_async_remote_copy(
                src_ref=out.at[ys[dy] * NZ + zs[dz]],
                dst_ref=got.at[me],
                send_sem=send.at[n],
                recv_sem=recv.at[n],
                device_id=(r, ys[dy], zs[dz]),
                device_id_type=MESH,
            )
            for n, (dy, dz) in enumerate(PLANE_STEPS)
        ]

    a_copies = plane_copies(a_out, a_got, a_send, a_recv)
    for copy in a_copies:
        copy.start()
    a_got[me] = a_out[me]
    for copy in a_copies:
        copy.wait_recv()

    turned = jnp.transpose(
        jnp.concatenate([a_got[a] for a in range(PLANE)], axis=0)
    )
    values = jnp.concatenate([turned[:ROWS], turned[64 : 64 + ROWS]], axis=1)
    high = values.astype(BF16)
    low = (values - high.astype(F32)).astype(BF16)
    left = jnp.concatenate([high, low], axis=0)
    wanted = values[TARGET : TARGET + 1, :]
    count = rows((128, PLANE * ITEMS)).astype(F32)
    count2 = jnp.where(count < 64.0, count + 128.0, count + 64.0)
    half = lanes((32, 128)) < 64

    def table(row):
        here = wanted - (row * OWN).astype(F32)
        parts = []
        for at in (count, count2):
            right = jnp.where(at == here, 1.0, 0.0).astype(BF16)
            both = lax.dot_general(left, right, NT, preferred_element_type=F32)
            parts.append(both[:ROWS] + both[ROWS:])
        whole, mixed = parts
        mixed = jnp.concatenate([mixed, jnp.zeros((64 - ROWS, 128), F32)], axis=0)
        return jnp.concatenate([whole, jnp.where(half, mixed[:32], mixed[32:])], axis=0)

    r_copies = []
    for n, other in enumerate(row_of):
        r_out[n] = table(other)
        copy = pltpu.make_async_remote_copy(
            src_ref=r_out.at[n],
            dst_ref=r_got.at[n],
            send_sem=r_send.at[n],
            recv_sem=r_recv.at[n],
            device_id=(other, y, z),
            device_id_type=MESH,
        )
        copy.start()
        r_copies.append(copy)
    total = table(r)
    for n, copy in enumerate(r_copies):
        copy.wait_recv()
        total = total + r_got[n]
    whole, mixed = total[:ROWS], total[ROWS:]
    mixed = jnp.concatenate([mixed, roll(mixed, 64)], axis=0)
    c_out[:, :128] = whole[CORNER : CORNER + 8]
    c_out[:, 128:] = mixed[CORNER : CORNER + 8]

    c_copies = [
        pltpu.make_async_remote_copy(
            src_ref=c_out,
            dst_ref=c_got.at[r],
            send_sem=c_send.at[n],
            recv_sem=c_recv.at[n],
            device_id=(other, y, z),
            device_id_type=MESH,
        )
        for n, other in enumerate(row_of)
    ]
    for copy in c_copies:
        copy.start()
    c_got[r] = c_out[...]

    whole = jnp.concatenate([whole, jnp.zeros((64 - ROWS, 128), F32)], axis=0)
    second = jnp.where(lanes((64, 128)) < 32, roll(whole, 32), roll(mixed, 32))
    bricks = jnp.transpose(jnp.concatenate([whole, second], axis=0))
    for a in range(PLANE):
        b_out[a] = bricks[a : a + 1]
    b_copies = plane_copies(b_out, b_got, b_send, b_recv)
    for copy in b_copies:
        copy.start()
    b_got[me] = b_out[me]

    for copy in c_copies:
        copy.wait_recv()
    kept, added = [], []
    for b in range(2):
        means = []
        for h in range(2):
            ref = refs_ref[b, :, h * 128 : h * 128 + 128]
            corner, brick = ref & 7, ref >> 3
            source = ((brick >> 6) * 11) >> 5
            place = brick - source * OWN
            place = (place >> 1) + (place & 1) * PLANE
            at = place & 127
            which = (source * 2 + (place >> 7)) * 8 + corner
            found = jnp.zeros((8, 128), F32)
            for n in range(NR):
                for part in range(2):
                    for c in range(8):
                        line = jnp.broadcast_to(
                            c_got[n, c : c + 1, part * 128 : part * 128 + 128], (8, 128)
                        )
                        here = jnp.take_along_axis(line, at, axis=1)
                        found = jnp.where(which == (n * 2 + part) * 8 + c, here, found)
            means.append(jnp.sum(found, axis=0, keepdims=True) * 0.0625)
        mean = jnp.concatenate(means, axis=1)
        cell = cell_ref[b : b + 1, :]
        upper = rows((32, 256)) == (cell >> 7)
        coarse = mean.astype(BF16).astype(F32)
        weights = jnp.concatenate(
            [
                jnp.where(upper, coarse, 0.0),
                jnp.where(upper, mean - coarse, 0.0),
                jnp.where(upper, 0.5, 0.0),
            ],
            axis=0,
        ).astype(BF16)
        spots = jnp.where(rows((128, 256)) == (cell & 127), 1.0, 0.0).astype(BF16)
        spread = lax.dot_general(weights, spots, NT, preferred_element_type=F32)
        added.append(spread[:32] + spread[32:64])
        kept.append(1.0 - spread[64:])

    for copy in b_copies:
        copy.wait_recv()
    lane = lanes((1, 128))
    for b in range(2):
        for t in range(PTS // 128):
            value = None
            for a in range(PLANE):
                first = a * SUB - t * 128
                if first < 128 and first + SUB > 0:
                    moved = roll(b_got[a], first - 64 * b)
                    value = moved if value is None else jnp.where(lane < first, value, moved)
            out_ref[b : b + 1, t * 128 : t * 128 + 128] = (
                value * kept[b][t : t + 1] + added[b][t : t + 1]
            )
    for copies in (a_copies, r_copies, b_copies, c_copies):
        for copy in copies:
            copy.wait_send()


def body(
    block_data, item_pairs, dest_slot, brick_tag, centres, exponents, levels, cell_pos, corner_refs
):
    arguments = (
        item_pairs.T,
        dest_slot,
        brick_tag,
        levels,
        centres.transpose(1, 0, 2),
        exponents,
        block_data,
        corner_refs.transpose(0, 2, 1),
        cell_pos,
    )
    places = [pltpu.SMEM] * 4 + [pltpu.VMEM] * 5
    dma = pltpu.SemaphoreType.DMA
    return pl.pallas_call(
        kernel,
        out_shape=jax.ShapeDtypeStruct((2, PTS), F32),
        in_specs=[pl.BlockSpec(memory_space=pltpu.HBM)] * len(arguments),
        out_specs=pl.BlockSpec(memory_space=pltpu.VMEM),
        scratch_shapes=[place(a.shape, a.dtype) for place, a in zip(places, arguments)]
        + [
            pltpu.VMEM((ITEMS, 34 * 128), F32),
            pltpu.VMEM((PLANE, 4, 128), F32),
            pltpu.VMEM((PLANE, 4, 128), F32),
            pltpu.VMEM((NR - 1, ROWS + 32, 128), F32),
            pltpu.VMEM((NR - 1, ROWS + 32, 128), F32),
            pltpu.VMEM((PLANE, 1, 128), F32),
            pltpu.VMEM((PLANE, 1, 128), F32),
            pltpu.VMEM((8, 256), F32),
            pltpu.VMEM((NR, 8, 256), F32),
            dma((len(arguments),)),
            pltpu.SemaphoreType.REGULAR,
            dma((PLANE - 1,)),
            dma((PLANE - 1,)),
            dma((NR - 1,)),
            dma((NR - 1,)),
            dma((PLANE - 1,)),
            dma((PLANE - 1,)),
            dma((NR - 1,)),
            dma((NR - 1,)),
        ],
        compiler_params=pltpu.CompilerParams(
            collective_id=0, has_side_effects=True, vmem_limit_bytes=60 * 2**20
        ),
        name="collocate",
    )(*arguments)


def solution(mesh):
    spread = ("row", "col", "basis")
    return jax.shard_map(
        body,
        mesh=mesh,
        in_specs=(
            P(spread, None, None),
            P(spread, None),
            P(spread),
            P(spread),
            P(),
            P(),
            P(),
            P(spread, None),
            P(spread, None, None),
        ),
        out_specs=P(spread, None),
        check_vma=False,
    )
```

time: 486 us -> 54.1 us (0.11); the launches traced: 479 us -> 53.9 us
  local copies, waits for them, and re-layouts: 142 us -> 1.38 us
  waiting for transfers between devices: 130 us -> 0 us
  blocking collectives: 99.8 us -> 0 us
  Pallas kernels: 0 us -> 52.5 us
  loops' own time: 33.4 us -> 0 us
  starting transfers between devices: 25 us -> 0 us
  other arithmetic: 22.4 us -> 0 us
  between operations: 14.3 us -> 0.01 us
  matrix products: 11.6 us -> 0 us
    unnamed x2 -> x0, waiting for transfers between devices: 105 us -> none
    all_gather x1 -> x0, blocking collectives: 99.8 us -> none  [body(): lax.all_gather(corner_values, ('row', 'col', 'basis'), axis=0, tiled=True)]
    scatter x3 -> x0, local copies, waits for them, and re-layouts: 68.2 us -> none  [the longest x1 66.7 us: body(): own_density.at[brick_rows, cell_pos].set(0.5 * current + 0.5 * corner_mean)]
    pallas_call x0 -> x1, Pallas kernels: none -> 52.5 us  [body(): pl.pallas_call(kernel, out_shape=jax.ShapeDtypeStruct((2, PTS), F32), in_...]
    another operation x1 -> x0, loops' own time: 33.4 us -> none  [body(): densities = lax.map(single, (block_data, item_pairs, item_level))]
    gather x7 -> x0, local copies, waits for them, and re-layouts: 29.3 us -> none  [the longest x2 23.2 us: body(): corner_mean = jnp.mean(all_corners[corner_refs], axis=-1)]
    all_to_all x2 -> x0, waiting for transfers between devices: 25.2 us -> none  [the longest x1 25.2 us: body(): lax.all_to_all(outgoing, ('row', 'col'), split_axis=0, concat_axis=0, til...]
    all_to_all x2 -> x0, starting transfers between devices: 24.9 us -> none  [the longest x1 14.6 us: body(): lax.all_to_all(slot_tags, ('row', 'col'), split_axis=0, concat_axis=0, ti...]
  transfers between devices with their start and end apart: 3 -> 0, of which waited for: 2 -> 0; matrix products, arithmetic and copies ran while one was open for 15% -> 0% of each run, Pallas kernels for 0% -> 0%
where the time goes in v2:
time: 54.1 us; the launch traced here: 53.9 us
  Pallas kernels  52.5 us (97%)
  local copies, waits for them, and re-layouts  1.38 us (3%)
    pallas_call x1, Pallas kernels, body(): pl.pallas_call(kernel, out_shape=jax.ShapeDtypeStruct((2, PTS), F32), in_...  52.5 us
    unnamed x1, local copies, waits for them, and re-layouts  1.38 us

profile of v2, /device:TPU:1, one launch (start us, length us, event | category | flops | bytes accessed | tf_op | source)
XLA Modules:
  0.0 53.9 jit_solution(8959943802376294180)
XLA Ops:
  0.0 52.5 %collocate.1 = f32[2,4096]{1,0:T(2,128)} custom-call(s32[2,8]{1,0:T(2,128)} %bitcast.5, s32[8]{0:T(128)} %slot_hbm.1, s32[8]{0:T(128)} %tag_hbm.1, s32[1536]{0:T(1024)} %levels_hbm.1, f32[3,1024,128]{2,1,0:T(8,128)} %bitcast.3, f32[1024,128]{1,0:T(8,128)} %exp_hbm.1, bf16[8,128,128]{2,1,0:T(8,128)(2,1)} %block_hbm.1, s32[2,8,256]{2,1,0:T(8,128)} %bitcast.4, ...), custom_call_target="tpu_custom_call" | custom-call | tf_op jit(solution)/shard_map/collocate/pallas_call | solution.py:367
  52.5 1.4 %copy.11 = f32[2,4096]{1,0:T(2,128)} copy(f32[2,4096]{1,0:T(2,128)} %collocate.1) | data formatting | bytes 65536

commit v3 on v2

--- a/solution.py
+++ b/solution.py
@@ -135,7 +135,6 @@
     step_y = (lane256 // EDGE).astype(F32) - HALF
     step_z = (lane256 % EDGE).astype(F32) - HALF
     step_x = lanes((1, BS)).astype(F32) - HALF
-    dens_ref[:, PTS:] = jnp.zeros((ITEMS, dens_ref.shape[1] - PTS), F32)
     for load in loads:
         load.wait()
 
@@ -188,36 +187,39 @@
     for c, q in enumerate(CORNERS):
         tile = dens_ref[:, q // 128 * 128 : q // 128 * 128 + 128]
         extra = jnp.where(lane == CORNER + c, roll(tile, CORNER + c - q), extra)
-    half = lanes((4, 128)) < 64
-    for a in range(PLANE):
-        tile, shift = a * SUB // 128, a * SUB % 128
-        value = roll(dens_ref[:, tile * 128 : tile * 128 + 128], -shift)
-        if shift + SUB > 128:
-            after = roll(dens_ref[:, tile * 128 + 128 : tile * 128 + 256], -shift)
-            value = jnp.where(lane < 128 - shift, value, after)
-        value = jnp.where(lane < SUB, value, extra)
-        a_out[a] = jnp.where(half, value[:4], roll(value, 64)[4:])
+    lower = lane < 64
+
+    def beside(x):
+        return pltpu.roll(roll(x, 64), 4, 0)
+
+    extra = jnp.where(lower, extra, beside(extra))
+    point = (lane & 63) < SUB
+    for t in range(PTS // 128):
+        tile = dens_ref[:, t * 128 : t * 128 + 128]
+        other = beside(tile)
+        for m in range(3):
+            value = jnp.where(lower, roll(tile, -SUB * m), roll(other, -SUB * m))
+            a_out[3 * t + m] = jnp.where(point, value, extra)[:4]
     pl.semaphore_wait(again_sem, NC - 1)
 
     def plane_copies(out, got, send, recv):
-        return [
+        for dy, dz in PLANE_STEPS:
             pltpu.make_async_remote_copy(
                 src_ref=out.at[ys[dy] * NZ + zs[dz]],
                 dst_ref=got.at[me],
-                send_sem=send.at[n],
-                recv_sem=recv.at[n],
+                send_sem=send,
+                recv_sem=recv,
                 device_id=(r, ys[dy], zs[dz]),
                 device_id_type=MESH,
-            )
-            for n, (dy, dz) in enumerate(PLANE_STEPS)
-        ]
-
-    a_copies = plane_copies(a_out, a_got, a_send, a_recv)
-    for copy in a_copies:
-        copy.start()
-    a_got[me] = a_out[me]
-    for copy in a_copies:
-        copy.wait_recv()
+            ).start()
+        got[me] = out[me]
+
+    def arrived(ref, count, sem):
+        whole = ref.at[pl.ds(0, count)]
+        pltpu.make_async_copy(whole, whole, sem).wait()
+
+    plane_copies(a_out, a_got, a_send, a_recv)
+    arrived(a_got, PLANE - 1, a_recv)
 
     turned = jnp.transpose(
         jnp.concatenate([a_got[a] for a in range(PLANE)], axis=0)
@@ -242,41 +244,34 @@
         mixed = jnp.concatenate([mixed, jnp.zeros((64 - ROWS, 128), F32)], axis=0)
         return jnp.concatenate([whole, jnp.where(half, mixed[:32], mixed[32:])], axis=0)
 
-    r_copies = []
     for n, other in enumerate(row_of):
         r_out[n] = table(other)
-        copy = pltpu.make_async_remote_copy(
+        pltpu.make_async_remote_copy(
             src_ref=r_out.at[n],
             dst_ref=r_got.at[n],
-            send_sem=r_send.at[n],
-            recv_sem=r_recv.at[n],
+            send_sem=r_send,
+            recv_sem=r_recv,
             device_id=(other, y, z),
             device_id_type=MESH,
-        )
-        copy.start()
-        r_copies.append(copy)
+        ).start()
     total = table(r)
-    for n, copy in enumerate(r_copies):
-        copy.wait_recv()
+    arrived(r_got, NR - 1, r_recv)
+    for n in range(NR - 1):
         total = total + r_got[n]
     whole, mixed = total[:ROWS], total[ROWS:]
     mixed = jnp.concatenate([mixed, roll(mixed, 64)], axis=0)
     c_out[:, :128] = whole[CORNER : CORNER + 8]
     c_out[:, 128:] = mixed[CORNER : CORNER + 8]
 
-    c_copies = [
+    for other in row_of:
         pltpu.make_async_remote_copy(
             src_ref=c_out,
             dst_ref=c_got.at[r],
-            send_sem=c_send.at[n],
-            recv_sem=c_recv.at[n],
+            send_sem=c_send,
+            recv_sem=c_recv,
             device_id=(other, y, z),
             device_id_type=MESH,
-        )
-        for n, other in enumerate(row_of)
-    ]
-    for copy in c_copies:
-        copy.start()
+        ).start()
     c_got[r] = c_out[...]
 
     whole = jnp.concatenate([whole, jnp.zeros((64 - ROWS, 128), F32)], axis=0)
@@ -284,13 +279,9 @@
     bricks = jnp.transpose(jnp.concatenate([whole, second], axis=0))
     for a in range(PLANE):
         b_out[a] = bricks[a : a + 1]
-    b_copies = plane_copies(b_out, b_got, b_send, b_recv)
-    for copy in b_copies:
-        copy.start()
-    b_got[me] = b_out[me]
-
-    for copy in c_copies:
-        copy.wait_recv()
+    plane_copies(b_out, b_got, b_send, b_recv)
+
+    arrived(c_got, NR - 1, c_recv)
     kept, added = [], []
     for b in range(2):
         means = []
@@ -329,23 +320,21 @@
         added.append(spread[:32] + spread[32:64])
         kept.append(1.0 - spread[64:])
 
-    for copy in b_copies:
-        copy.wait_recv()
+    arrived(b_got, PLANE - 1, b_recv)
     lane = lanes((1, 128))
     for b in range(2):
         for t in range(PTS // 128):
-            value = None
-            for a in range(PLANE):
-                first = a * SUB - t * 128
-                if first < 128 and first + SUB > 0:
-                    moved = roll(b_got[a], first - 64 * b)
-                    value = moved if value is None else jnp.where(lane < first, value, moved)
+            thirds = [roll(b_got[3 * t + m], SUB * m - 64 * b) for m in range(3)]
+            value = jnp.where(
+                lane < SUB, thirds[0], jnp.where(lane < 2 * SUB, thirds[1], thirds[2])
+            )
             out_ref[b : b + 1, t * 128 : t * 128 + 128] = (
                 value * kept[b][t : t + 1] + added[b][t : t + 1]
             )
-    for copies in (a_copies, r_copies, b_copies, c_copies):
-        for copy in copies:
-            copy.wait_send()
+    arrived(a_out, PLANE - 1, a_send)
+    arrived(r_out, NR - 1, r_send)
+    arrived(b_out, PLANE - 1, b_send)
+    arrived(c_got, NR - 1, c_send)
 
 
 def body(
@@ -366,12 +355,12 @@
     dma = pltpu.SemaphoreType.DMA
     return pl.pallas_call(
         kernel,
-        out_shape=jax.ShapeDtypeStruct((2, PTS), F32),
+        out_shape=pltpu.VMEM((2, PTS), F32),
         in_specs=[pl.BlockSpec(memory_space=pltpu.HBM)] * len(arguments),
         out_specs=pl.BlockSpec(memory_space=pltpu.VMEM),
         scratch_shapes=[place(a.shape, a.dtype) for place, a in zip(places, arguments)]
         + [
-            pltpu.VMEM((ITEMS, 34 * 128), F32),
+            pltpu.VMEM((ITEMS, PTS), F32),
             pltpu.VMEM((PLANE, 4, 128), F32),
             pltpu.VMEM((PLANE, 4, 128), F32),
             pltpu.VMEM((NR - 1, ROWS + 32, 128), F32),
@@ -382,15 +371,8 @@
             pltpu.VMEM((NR, 8, 256), F32),
             dma((len(arguments),)),
             pltpu.SemaphoreType.REGULAR,
-            dma((PLANE - 1,)),
-            dma((PLANE - 1,)),
-            dma((NR - 1,)),
-            dma((NR - 1,)),
-            dma((PLANE - 1,)),
-            dma((PLANE - 1,)),
-            dma((NR - 1,)),
-            dma((NR - 1,)),
-        ],
+        ]
+        + [dma] * 8,
         compiler_params=pltpu.CompilerParams(
             collective_id=0, has_side_effects=True, vmem_limit_bytes=60 * 2**20
         ),

time: 54.1 us -> 47.7 us (0.88)
  Pallas kernels: 52.5 us -> 47 us
  local copies, waits for them, and re-layouts: 1.38 us -> 0.62 us
    pallas_call x1, Pallas kernels: 52.5 us -> 47 us  [body(): pl.pallas_call(kernel, out_shape=pltpu.VMEM((2, PTS), F32), in_specs=[pl....]
    unnamed x1, local copies, waits for them, and re-layouts: 1.38 us -> 0.62 us
where the time goes in v3:
time: 47.7 us; the launch traced here: 47.6 us
  Pallas kernels  47 us (99%)
  local copies, waits for them, and re-layouts  0.62 us (1%)
    pallas_call x1, Pallas kernels, body(): pl.pallas_call(kernel, out_shape=pltpu.VMEM((2, PTS), F32), in_specs=[pl....  47 us

profile of v3, /device:TPU:1, one launch (start us, length us, event | category | flops | bytes accessed | tf_op | source)
XLA Modules:
  0.0 47.6 jit_solution(4372789324178727529)
XLA Ops:
  0.0 47.0 %collocate.1 = f32[2,4096]{1,0:T(2,128)S(1)} custom-call(s32[2,8]{1,0:T(2,128)} %bitcast.5, s32[8]{0:T(128)} %slot_hbm.1, s32[8]{0:T(128)} %tag_hbm.1, s32[1536]{0:T(1024)} %levels_hbm.1, f32[3,1024,128]{2,1,0:T(8,128)} %bitcast.3, f32[1024,128]{1,0:T(8,128)} %exp_hbm.1, bf16[8,128,128]{2,1,0:T(8,128)(2,1)} %block_hbm.1, s32[2,8,256]{2,1,0:T(8,128)} %bitcast.4, ...), custom_call_target="tpu_custom_call" | custom-call | tf_op jit(solution)/shard_map/collocate/pallas_call | solution.py:356
  47.0 0.6 %copy.11 = f32[2,4096]{1,0:T(2,128)} copy(f32[2,4096]{1,0:T(2,128)S(1)} %collocate.1) | data formatting | bytes 65536

commit v4 on v3

--- a/solution.py
+++ b/solution.py
@@ -74,6 +74,10 @@
     block_ref,
     refs_ref,
     cell_ref,
+    colx_ref,
+    colyz_ref,
+    rowx_ref,
+    rowyz_ref,
     dens_ref,
     a_out,
     a_got,
@@ -110,9 +114,6 @@
             )
         )
     ]
-    for load in loads:
-        load.start()
-
     r, y, z = (lax.axis_index(a) for a in ("row", "col", "basis"))
     ys = [lax.rem(y + n, NC) for n in range(NC)]
     zs = [lax.rem(z + n, NZ) for n in range(NZ)]
@@ -123,66 +124,85 @@
     me = y * NZ + z
 
     barrier = pltpu.get_barrier_semaphore()
-    for n in range(1, NZ):
-        pl.semaphore_signal(barrier, inc=1, device_id=(r, y, zs[n]), device_id_type=MESH)
-    for n in range(1, NC):
-        pl.semaphore_signal(barrier, inc=1, device_id=(r, ys[n], z), device_id_type=MESH)
+
+    def entered(*device):
+        pl.semaphore_signal(barrier, inc=1, device_id=device, device_id_type=MESH)
+
+    col_steps = sorted(range(1, NC), key=lambda n: -far(n, NC))
+    for n in col_steps:
+        entered(r, ys[n], z)
+    for load in loads:
+        load.start()
+    for n in sorted(range(1, NZ), key=lambda n: -far(n, NZ)):
+        entered(r, y, zs[n])
     for other in row_of:
-        pl.semaphore_signal(barrier, inc=1, device_id=(other, y, z), device_id_type=MESH)
+        entered(other, y, z)
 
     step16 = rows((EDGE, BS)).astype(F32) - HALF
     lane256 = lanes((1, EDGE * EDGE))
     step_y = (lane256 // EDGE).astype(F32) - HALF
     step_z = (lane256 % EDGE).astype(F32) - HALF
-    step_x = lanes((1, BS)).astype(F32) - HALF
+    lane = lanes((ITEMS, 128))
     for load in loads:
         load.wait()
 
-    def item(k, targets):
+    numbers = jnp.zeros((ITEMS, 128), F32)
+    spacings, params, row_xs = [], [], []
+    for k in range(ITEMS):
         first, second = pairs_ref[0, k], pairs_ref[1, k]
         group, tag = slot_ref[k], tag_ref[k]
         spacing = jnp.where(levels_ref[group * GROUP + tag] == 0, 0.2, 0.1).astype(F32)
-
+        spacings.append(spacing)
+        place = (group & 7) * GROUP + tag
+        number = (group >> 3) * OWN + (place & 1) * PLANE + (place >> 1)
+        numbers = jnp.where(rows((ITEMS, 128)) == k, number.astype(F32), numbers)
+
+        points = step16 * spacing
         rate = exp_ref[pl.ds(second, 1), :]
         middle = [cen_ref[d, pl.ds(second, 1), :] for d in range(3)]
-        col_x, col_y, col_z = [jnp.exp(-rate * (step16 * spacing - m) ** 2) for m in middle]
-        col_yz = jnp.concatenate([col_y[n : n + 1] * col_z for n in range(EDGE)], axis=0)
-
-        params = jnp.concatenate(
-            [exp_ref[pl.ds(first, 1), :]]
-            + [cen_ref[d, pl.ds(first, 1), :] for d in range(3)]
-            + [jnp.zeros((4, BS), F32)],
-            axis=0,
-        )
-        columns = jnp.transpose(params)
-        decay = -columns[:, 0:1]
-        row_x = jnp.exp(decay * (step_x * spacing - columns[:, 1:2]) ** 2)
-        row_yz = jnp.exp(
+        col_x, col_y, col_z = [jnp.exp(-rate * (points - m) ** 2) for m in middle]
+        colx_ref[k] = col_x
+        for n in range(EDGE):
+            colyz_ref[k, n * EDGE : n * EDGE + EDGE, :] = col_y[n : n + 1] * col_z
+
+        rate = exp_ref[pl.ds(first, 1), :]
+        middle = [cen_ref[d, pl.ds(first, 1), :] for d in range(3)]
+        row_xs.append(jnp.exp(-rate * (points - middle[0]) ** 2))
+        params += [-rate, middle[1], middle[2]]
+    columns = jnp.transpose(
+        jnp.concatenate(params + [jnp.zeros((32 - 3 * ITEMS, BS), F32)], axis=0)
+    )
+    row_x = jnp.transpose(jnp.concatenate(row_xs, axis=0))
+    for k in range(ITEMS):
+        rowx_ref[k] = roll(row_x, -EDGE * k)
+        decay, middle_y, middle_z = (columns[:, 3 * k + n : 3 * k + n + 1] for n in range(3))
+        rowyz_ref[k] = jnp.exp(
             decay
             * (
-                (step_y * spacing - columns[:, 2:3]) ** 2
-                + (step_z * spacing - columns[:, 3:4]) ** 2
+                (step_y * spacings[k] - middle_y) ** 2
+                + (step_z * spacings[k] - middle_z) ** 2
             )
         )
+
+    def item(k, carry):
         block = block_ref[k]
+        col_x = colx_ref[k]
+        row_x = rowx_ref[k]
         for n in range(EDGE):
-            col_values = (col_x[n : n + 1] * col_yz).astype(BF16)
+            col_values = (col_x[n : n + 1] * colyz_ref[k]).astype(BF16)
             product = lax.dot_general(block, col_values, NT, preferred_element_type=F32)
-            weighted = product * row_yz * row_x[:, n : n + 1]
+            weighted = product * rowyz_ref[k] * row_x[:, n : n + 1]
             dens_ref[pl.ds(k, 1), n * 256 : n * 256 + 256] = jnp.sum(
                 weighted, axis=0, keepdims=True
             )
-        place = (group & 7) * GROUP + tag
-        number = (group >> 3) * OWN + (place & 1) * PLANE + (place >> 1)
-        return jnp.where(rows((ITEMS, 128)) == k, number.astype(F32), targets)
-
-    numbers = lax.fori_loop(0, ITEMS // 2, item, jnp.zeros((ITEMS, 128), F32))
+        return carry
+
+    lax.fori_loop(0, ITEMS // 2, item, 0, unroll=True)
     pl.semaphore_wait(barrier, NR + NC + NZ - 3)
-    for n in range(1, NC):
+    for n in col_steps:
         pl.semaphore_signal(again_sem, inc=1, device_id=(r, ys[n], z), device_id_type=MESH)
-    numbers = lax.fori_loop(ITEMS // 2, ITEMS, item, numbers)
-
-    lane = lanes((ITEMS, 128))
+    lax.fori_loop(ITEMS // 2, ITEMS, item, 0, unroll=True)
+
     extra = jnp.where(lane == TARGET, numbers, 0.0)
     for c, q in enumerate(CORNERS):
         tile = dens_ref[:, q // 128 * 128 : q // 128 * 128 + 128]
@@ -360,6 +380,10 @@
         out_specs=pl.BlockSpec(memory_space=pltpu.VMEM),
         scratch_shapes=[place(a.shape, a.dtype) for place, a in zip(places, arguments)]
         + [
+            pltpu.VMEM((ITEMS, EDGE, BS), F32),
+            pltpu.VMEM((ITEMS, EDGE * EDGE, BS), F32),
+            pltpu.VMEM((ITEMS, BS, 128), F32),
+            pltpu.VMEM((ITEMS, BS, EDGE * EDGE), F32),
             pltpu.VMEM((ITEMS, PTS), F32),
             pltpu.VMEM((PLANE, 4, 128), F32),
             pltpu.VMEM((PLANE, 4, 128), F32),

time: 47.7 us -> 47.3 us (level)
  Pallas kernels: 47 us -> 46.5 us
    pallas_call x1, Pallas kernels: 47 us -> 46.5 us  [body(): pl.pallas_call(kernel, out_shape=pltpu.VMEM((2, PTS), F32), in_specs=[pl....]
where the time goes in v4:
time: 47.3 us; the launch traced here: 47.1 us
  Pallas kernels  46.5 us (98%)
  local copies, waits for them, and re-layouts  0.62 us (1%)
    pallas_call x1, Pallas kernels, body(): pl.pallas_call(kernel, out_shape=pltpu.VMEM((2, PTS), F32), in_specs=[pl....  46.5 us

profile of v4, /device:TPU:1, one launch (start us, length us, event | category | flops | bytes accessed | tf_op | source)
XLA Modules:
  0.0 47.1 jit_solution(16301811864126632269)
XLA Ops:
  0.0 46.5 %collocate.1 = f32[2,4096]{1,0:T(2,128)S(1)} custom-call(s32[2,8]{1,0:T(2,128)} %bitcast.5, s32[8]{0:T(128)} %slot_hbm.1, s32[8]{0:T(128)} %tag_hbm.1, s32[1536]{0:T(1024)} %levels_hbm.1, f32[3,1024,128]{2,1,0:T(8,128)} %bitcast.3, f32[1024,128]{1,0:T(8,128)} %exp_hbm.1, bf16[8,128,128]{2,1,0:T(8,128)(2,1)} %block_hbm.1, s32[2,8,256]{2,1,0:T(8,128)} %bitcast.4, ...), custom_call_target="tpu_custom_call" | custom-call | tf_op jit(solution)/shard_map/collocate/pallas_call | solution.py:376
  46.5 0.6 %copy.11 = f32[2,4096]{1,0:T(2,128)} copy(f32[2,4096]{1,0:T(2,128)S(1)} %collocate.1) | data formatting | bytes 65536

commit v5 on v4

--- a/solution.py
+++ b/solution.py
@@ -17,6 +17,7 @@
 BS = 128
 ITEMS = 8
 NR, NC, NZ = 8, 8, 12
+NX = NR // 2
 PLANE = NC * NZ
 GROUP = 24
 OWN = NC * GROUP
@@ -38,6 +39,7 @@
     (s for s in itertools.product(range(NC), range(NZ)) if any(s)),
     key=lambda s: -(far(s[0], NC) + far(s[1], NZ)),
 )
+CHIP_STEPS = (2, 1, 3, 0)
 ROW_STEPS = ((2, 1), (2, 0), (1, 1), (3, 1), (1, 0), (3, 0), (0, 1))
 
 
@@ -81,6 +83,8 @@
     dens_ref,
     a_out,
     a_got,
+    h_out,
+    h_got,
     r_out,
     r_got,
     b_out,
@@ -91,6 +95,8 @@
     again_sem,
     a_send,
     a_recv,
+    h_send,
+    h_recv,
     r_send,
     r_recv,
     b_send,
@@ -118,7 +124,7 @@
     ys = [lax.rem(y + n, NC) for n in range(NC)]
     zs = [lax.rem(z + n, NZ) for n in range(NZ)]
     x, core = r // 2, lax.rem(r, 2)
-    xs = [lax.rem(x + n, NR // 2) * 2 for n in range(NR // 2)]
+    xs = [lax.rem(x + n, NX) * 2 for n in range(NX)]
     cores = [core, 1 - core]
     row_of = [xs[dx] + cores[dc] for dx, dc in ROW_STEPS]
     me = y * NZ + z
@@ -264,25 +270,49 @@
         mixed = jnp.concatenate([mixed, jnp.zeros((64 - ROWS, 128), F32)], axis=0)
         return jnp.concatenate([whole, jnp.where(half, mixed[:32], mixed[32:])], axis=0)
 
-    for n, other in enumerate(row_of):
-        r_out[n] = table(other)
+    halves = []
+    for n, dx in enumerate(CHIP_STEPS):
+        h_out[n] = table(xs[dx] + cores[1])
+        half_copy = pltpu.make_async_remote_copy(
+            src_ref=h_out.at[n],
+            dst_ref=h_got.at[n],
+            send_sem=h_send,
+            recv_sem=h_recv.at[n],
+            device_id=(xs[0] + cores[1], y, z),
+            device_id_type=MESH,
+        )
+        half_copy.start()
+        halves.append(half_copy)
+    for n, dx in enumerate(CHIP_STEPS):
+        r_out[n] = table(xs[dx] + core)
+    for n, dx in enumerate(CHIP_STEPS[:-1]):
+        halves[n].wait_recv()
+        r_out[n] = r_out[n] + h_got[n]
         pltpu.make_async_remote_copy(
             src_ref=r_out.at[n],
             dst_ref=r_got.at[n],
             send_sem=r_send,
             recv_sem=r_recv,
-            device_id=(other, y, z),
+            device_id=(xs[dx] + core, y, z),
             device_id_type=MESH,
         ).start()
-    total = table(r)
-    arrived(r_got, NR - 1, r_recv)
-    for n in range(NR - 1):
+    halves[-1].wait_recv()
+    total = r_out[NX - 1] + h_got[NX - 1]
+    arrived(r_got, NX - 1, r_recv)
+    for n in range(NX - 1):
         total = total + r_got[n]
     whole, mixed = total[:ROWS], total[ROWS:]
     mixed = jnp.concatenate([mixed, roll(mixed, 64)], axis=0)
+
+    whole = jnp.concatenate([whole, jnp.zeros((64 - ROWS, 128), F32)], axis=0)
+    second = jnp.where(lanes((64, 128)) < 32, roll(whole, 32), roll(mixed, 32))
+    bricks = jnp.transpose(jnp.concatenate([whole, second], axis=0))
+    for a in range(PLANE):
+        b_out[a] = bricks[a : a + 1]
+    plane_copies(b_out, b_got, b_send, b_recv)
+
     c_out[:, :128] = whole[CORNER : CORNER + 8]
     c_out[:, 128:] = mixed[CORNER : CORNER + 8]
-
     for other in row_of:
         pltpu.make_async_remote_copy(
             src_ref=c_out,
@@ -293,13 +323,6 @@
             device_id_type=MESH,
         ).start()
     c_got[r] = c_out[...]
-
-    whole = jnp.concatenate([whole, jnp.zeros((64 - ROWS, 128), F32)], axis=0)
-    second = jnp.where(lanes((64, 128)) < 32, roll(whole, 32), roll(mixed, 32))
-    bricks = jnp.transpose(jnp.concatenate([whole, second], axis=0))
-    for a in range(PLANE):
-        b_out[a] = bricks[a : a + 1]
-    plane_copies(b_out, b_got, b_send, b_recv)
 
     arrived(c_got, NR - 1, c_recv)
     kept, added = [], []
@@ -352,7 +375,8 @@
                 value * kept[b][t : t + 1] + added[b][t : t + 1]
             )
     arrived(a_out, PLANE - 1, a_send)
-    arrived(r_out, NR - 1, r_send)
+    arrived(h_out, NX, h_send)
+    arrived(r_out, NX - 1, r_send)
     arrived(b_out, PLANE - 1, b_send)
     arrived(c_got, NR - 1, c_send)
 
@@ -387,8 +411,10 @@
             pltpu.VMEM((ITEMS, PTS), F32),
             pltpu.VMEM((PLANE, 4, 128), F32),
             pltpu.VMEM((PLANE, 4, 128), F32),
-            pltpu.VMEM((NR - 1, ROWS + 32, 128), F32),
-            pltpu.VMEM((NR - 1, ROWS + 32, 128), F32),
+            pltpu.VMEM((NX, ROWS + 32, 128), F32),
+            pltpu.VMEM((NX, ROWS + 32, 128), F32),
+            pltpu.VMEM((NX, ROWS + 32, 128), F32),
+            pltpu.VMEM((NX - 1, ROWS + 32, 128), F32),
             pltpu.VMEM((PLANE, 1, 128), F32),
             pltpu.VMEM((PLANE, 1, 128), F32),
             pltpu.VMEM((8, 256), F32),
@@ -396,7 +422,8 @@
             dma((len(arguments),)),
             pltpu.SemaphoreType.REGULAR,
         ]
-        + [dma] * 8,
+        + [dma, dma, dma, dma((NX,))]
+        + [dma] * 6,
         compiler_params=pltpu.CompilerParams(
             collective_id=0, has_side_effects=True, vmem_limit_bytes=60 * 2**20
         ),

time: 47.3 us -> 47.7 us (level)
  no operation moved by 1% of the time
where the time goes in v5:
time: 47.7 us; the launch traced here: 47.5 us
  Pallas kernels  46.9 us (98%)
  local copies, waits for them, and re-layouts  0.62 us (1%)
    pallas_call x1, Pallas kernels, body(): pl.pallas_call(kernel, out_shape=pltpu.VMEM((2, PTS), F32), in_specs=[pl....  46.9 us

profile of v5, /device:TPU:1, one launch (start us, length us, event | category | flops | bytes accessed | tf_op | source)
XLA Modules:
  0.0 47.5 jit_solution(13398446385173441920)
XLA Ops:
  0.0 46.9 %collocate.1 = f32[2,4096]{1,0:T(2,128)S(1)} custom-call(s32[2,8]{1,0:T(2,128)} %bitcast.5, s32[8]{0:T(128)} %slot_hbm.1, s32[8]{0:T(128)} %tag_hbm.1, s32[1536]{0:T(1024)} %levels_hbm.1, f32[3,1024,128]{2,1,0:T(8,128)} %bitcast.3, f32[1024,128]{1,0:T(8,128)} %exp_hbm.1, bf16[8,128,128]{2,1,0:T(8,128)(2,1)} %block_hbm.1, s32[2,8,256]{2,1,0:T(8,128)} %bitcast.4, ...), custom_call_target="tpu_custom_call" | custom-call | tf_op jit(solution)/shard_map/collocate/pallas_call | solution.py:400
  46.9 0.6 %copy.11 = f32[2,4096]{1,0:T(2,128)} copy(f32[2,4096]{1,0:T(2,128)S(1)} %collocate.1) | data formatting | bytes 65536

commit v6 on v5

--- a/solution.py
+++ b/solution.py
@@ -92,7 +92,6 @@
     c_out,
     c_got,
     load_sem,
-    again_sem,
     a_send,
     a_recv,
     h_send,
@@ -134,13 +133,10 @@
     def entered(*device):
         pl.semaphore_signal(barrier, inc=1, device_id=device, device_id_type=MESH)
 
-    col_steps = sorted(range(1, NC), key=lambda n: -far(n, NC))
-    for n in col_steps:
-        entered(r, ys[n], z)
     for load in loads:
         load.start()
-    for n in sorted(range(1, NZ), key=lambda n: -far(n, NZ)):
-        entered(r, y, zs[n])
+    for dy, dz in PLANE_STEPS:
+        entered(r, ys[dy], zs[dz])
     for other in row_of:
         entered(other, y, z)
 
@@ -204,9 +200,6 @@
         return carry
 
     lax.fori_loop(0, ITEMS // 2, item, 0, unroll=True)
-    pl.semaphore_wait(barrier, NR + NC + NZ - 3)
-    for n in col_steps:
-        pl.semaphore_signal(again_sem, inc=1, device_id=(r, ys[n], z), device_id_type=MESH)
     lax.fori_loop(ITEMS // 2, ITEMS, item, 0, unroll=True)
 
     extra = jnp.where(lane == TARGET, numbers, 0.0)
@@ -226,7 +219,7 @@
         for m in range(3):
             value = jnp.where(lower, roll(tile, -SUB * m), roll(other, -SUB * m))
             a_out[3 * t + m] = jnp.where(point, value, extra)[:4]
-    pl.semaphore_wait(again_sem, NC - 1)
+    pl.semaphore_wait(barrier, PLANE + NR - 2)
 
     def plane_copies(out, got, send, recv):
         for dy, dz in PLANE_STEPS:
@@ -304,13 +297,6 @@
     whole, mixed = total[:ROWS], total[ROWS:]
     mixed = jnp.concatenate([mixed, roll(mixed, 64)], axis=0)
 
-    whole = jnp.concatenate([whole, jnp.zeros((64 - ROWS, 128), F32)], axis=0)
-    second = jnp.where(lanes((64, 128)) < 32, roll(whole, 32), roll(mixed, 32))
-    bricks = jnp.transpose(jnp.concatenate([whole, second], axis=0))
-    for a in range(PLANE):
-        b_out[a] = bricks[a : a + 1]
-    plane_copies(b_out, b_got, b_send, b_recv)
-
     c_out[:, :128] = whole[CORNER : CORNER + 8]
     c_out[:, 128:] = mixed[CORNER : CORNER + 8]
     for other in row_of:
@@ -323,6 +309,13 @@
             device_id_type=MESH,
         ).start()
     c_got[r] = c_out[...]
+
+    whole = jnp.concatenate([whole, jnp.zeros((64 - ROWS, 128), F32)], axis=0)
+    second = jnp.where(lanes((64, 128)) < 32, roll(whole, 32), roll(mixed, 32))
+    bricks = jnp.transpose(jnp.concatenate([whole, second], axis=0))
+    for a in range(PLANE):
+        b_out[a] = bricks[a : a + 1]
+    plane_copies(b_out, b_got, b_send, b_recv)
 
     arrived(c_got, NR - 1, c_recv)
     kept, added = [], []
@@ -420,7 +413,6 @@
             pltpu.VMEM((8, 256), F32),
             pltpu.VMEM((NR, 8, 256), F32),
             dma((len(arguments),)),
-            pltpu.SemaphoreType.REGULAR,
         ]
         + [dma, dma, dma, dma((NX,))]
         + [dma] * 6,

time: 47.7 us -> 47 us (0.985)
  Pallas kernels: 46.9 us -> 46.2 us
    pallas_call x1, Pallas kernels: 46.9 us -> 46.2 us  [body(): pl.pallas_call(kernel, out_shape=pltpu.VMEM((2, PTS), F32), in_specs=[pl....]
where the time goes in v6:
time: 47 us; the launch traced here: 46.8 us
  Pallas kernels  46.2 us (98%)
  local copies, waits for them, and re-layouts  0.62 us (1%)
    pallas_call x1, Pallas kernels, body(): pl.pallas_call(kernel, out_shape=pltpu.VMEM((2, PTS), F32), in_specs=[pl....  46.2 us

profile of v6, /device:TPU:1, one launch (start us, length us, event | category | flops | bytes accessed | tf_op | source)
XLA Modules:
  0.0 46.8 jit_solution(4551819386247386197)
XLA Ops:
  0.0 46.2 %collocate.1 = f32[2,4096]{1,0:T(2,128)S(1)} custom-call(s32[2,8]{1,0:T(2,128)} %bitcast.5, s32[8]{0:T(128)} %slot_hbm.1, s32[8]{0:T(128)} %tag_hbm.1, s32[1536]{0:T(1024)} %levels_hbm.1, f32[3,1024,128]{2,1,0:T(8,128)} %bitcast.3, f32[1024,128]{1,0:T(8,128)} %exp_hbm.1, bf16[8,128,128]{2,1,0:T(8,128)(2,1)} %block_hbm.1, s32[2,8,256]{2,1,0:T(8,128)} %bitcast.4, ...), custom_call_target="tpu_custom_call" | custom-call | tf_op jit(solution)/shard_map/collocate/pallas_call | solution.py:393
  46.2 0.6 %copy.11 = f32[2,4096]{1,0:T(2,128)} copy(f32[2,4096]{1,0:T(2,128)S(1)} %collocate.1) | data formatting | bytes 65536

commit v7 on v6

--- a/solution.py
+++ b/solution.py
@@ -19,6 +19,7 @@
 NR, NC, NZ = 8, 8, 12
 NX = NR // 2
 PLANE = NC * NZ
+BATCH = 24
 GROUP = 24
 OWN = NC * GROUP
 SUB = 43
@@ -81,6 +82,8 @@
     rowx_ref,
     rowyz_ref,
     dens_ref,
+    side_ref,
+    bricks_ref,
     a_out,
     a_got,
     h_out,
@@ -214,30 +217,42 @@
     extra = jnp.where(lower, extra, beside(extra))
     point = (lane & 63) < SUB
     for t in range(PTS // 128):
-        tile = dens_ref[:, t * 128 : t * 128 + 128]
-        other = beside(tile)
-        for m in range(3):
-            value = jnp.where(lower, roll(tile, -SUB * m), roll(other, -SUB * m))
-            a_out[3 * t + m] = jnp.where(point, value, extra)[:4]
-    pl.semaphore_wait(barrier, PLANE + NR - 2)
-
-    def plane_copies(out, got, send, recv):
-        for dy, dz in PLANE_STEPS:
-            pltpu.make_async_remote_copy(
-                src_ref=out.at[ys[dy] * NZ + zs[dz]],
-                dst_ref=got.at[me],
-                send_sem=send,
-                recv_sem=recv,
-                device_id=(r, ys[dy], zs[dz]),
-                device_id_type=MESH,
-            ).start()
-        got[me] = out[me]
+        side_ref[:, t * 128 : t * 128 + 128] = beside(dens_ref[:, t * 128 : t * 128 + 128])
+    tiles_y = [n * (NZ // 3) for n in ys]
+    tiles_z = [n // 3 for n in zs]
+    turns = [lax.rem(128 - SUB * lax.rem(n, 3), 128) for n in zs]
+
+    def chunk(dy, dz):
+        at = pl.ds(pl.multiple_of((tiles_y[dy] + tiles_z[dz]) * 128, 128), 128)
+        value = jnp.where(
+            lower,
+            pltpu.roll(dens_ref[:, at], turns[dz], 1),
+            pltpu.roll(side_ref[:, at], turns[dz], 1),
+        )
+        return jnp.where(point, value, extra)[:4]
+
+    def plane_copies(made, out, got, send, recv):
+        for begin in range(0, PLANE - 1, BATCH):
+            batch = list(enumerate(PLANE_STEPS))[begin : begin + BATCH]
+            for n, (dy, dz) in batch:
+                out[n] = made(dy, dz)
+            for n, (dy, dz) in batch:
+                pltpu.make_async_remote_copy(
+                    src_ref=out.at[n],
+                    dst_ref=got.at[me],
+                    send_sem=send,
+                    recv_sem=recv,
+                    device_id=(r, ys[dy], zs[dz]),
+                    device_id_type=MESH,
+                ).start()
+        got[me] = made(0, 0)
 
     def arrived(ref, count, sem):
         whole = ref.at[pl.ds(0, count)]
         pltpu.make_async_copy(whole, whole, sem).wait()
 
-    plane_copies(a_out, a_got, a_send, a_recv)
+    pl.semaphore_wait(barrier, PLANE + NR - 2)
+    plane_copies(chunk, a_out, a_got, a_send, a_recv)
     arrived(a_got, PLANE - 1, a_recv)
 
     turned = jnp.transpose(
@@ -312,10 +327,12 @@
 
     whole = jnp.concatenate([whole, jnp.zeros((64 - ROWS, 128), F32)], axis=0)
     second = jnp.where(lanes((64, 128)) < 32, roll(whole, 32), roll(mixed, 32))
-    bricks = jnp.transpose(jnp.concatenate([whole, second], axis=0))
-    for a in range(PLANE):
-        b_out[a] = bricks[a : a + 1]
-    plane_copies(b_out, b_got, b_send, b_recv)
+    bricks_ref[...] = jnp.transpose(jnp.concatenate([whole, second], axis=0))
+
+    def own_points(dy, dz):
+        return bricks_ref[pl.ds(ys[dy] * NZ + zs[dz], 1), :]
+
+    plane_copies(own_points, b_out, b_got, b_send, b_recv)
 
     arrived(c_got, NR - 1, c_recv)
     kept, added = [], []
@@ -402,13 +419,15 @@
             pltpu.VMEM((ITEMS, BS, 128), F32),
             pltpu.VMEM((ITEMS, BS, EDGE * EDGE), F32),
             pltpu.VMEM((ITEMS, PTS), F32),
-            pltpu.VMEM((PLANE, 4, 128), F32),
+            pltpu.VMEM((ITEMS, PTS), F32),
+            pltpu.VMEM((128, 128), F32),
+            pltpu.VMEM((PLANE - 1, 4, 128), F32),
             pltpu.VMEM((PLANE, 4, 128), F32),
             pltpu.VMEM((NX, ROWS + 32, 128), F32),
             pltpu.VMEM((NX, ROWS + 32, 128), F32),
             pltpu.VMEM((NX, ROWS + 32, 128), F32),
             pltpu.VMEM((NX - 1, ROWS + 32, 128), F32),
-            pltpu.VMEM((PLANE, 1, 128), F32),
+            pltpu.VMEM((PLANE - 1, 1, 128), F32),
             pltpu.VMEM((PLANE, 1, 128), F32),
             pltpu.VMEM((8, 256), F32),
             pltpu.VMEM((NR, 8, 256), F32),

time: 47 us -> 47.1 us (level)
  no operation moved by 1% of the time
where the time goes in v7:
time: 47.1 us; the launch traced here: 47 us
  Pallas kernels  46.3 us (98%)
  local copies, waits for them, and re-layouts  0.62 us (1%)
    pallas_call x1, Pallas kernels, body(): pl.pallas_call(kernel, out_shape=pltpu.VMEM((2, PTS), F32), in_specs=[pl....  46.3 us

profile of v7, /device:TPU:1, one launch (start us, length us, event | category | flops | bytes accessed | tf_op | source)
XLA Modules:
  0.0 47.0 jit_solution(1195234098002938488)
XLA Ops:
  0.0 46.3 %collocate.1 = f32[2,4096]{1,0:T(2,128)S(1)} custom-call(s32[2,8]{1,0:T(2,128)} %bitcast.5, s32[8]{0:T(128)} %slot_hbm.1, s32[8]{0:T(128)} %tag_hbm.1, s32[1536]{0:T(1024)} %levels_hbm.1, f32[3,1024,128]{2,1,0:T(8,128)} %bitcast.3, f32[1024,128]{1,0:T(8,128)} %exp_hbm.1, bf16[8,128,128]{2,1,0:T(8,128)(2,1)} %block_hbm.1, s32[2,8,256]{2,1,0:T(8,128)} %bitcast.4, ...), custom_call_target="tpu_custom_call" | custom-call | tf_op jit(solution)/shard_map/collocate/pallas_call | solution.py:410
  46.3 0.6 %copy.11 = f32[2,4096]{1,0:T(2,128)} copy(f32[2,4096]{1,0:T(2,128)S(1)} %collocate.1) | data formatting | bytes 65536

commit v8 on v7

--- a/solution.py
+++ b/solution.py
@@ -136,9 +136,11 @@
     def entered(*device):
         pl.semaphore_signal(barrier, inc=1, device_id=device, device_id_type=MESH)
 
+    for dy, dz in PLANE_STEPS[:BATCH]:
+        entered(r, ys[dy], zs[dz])
     for load in loads:
         load.start()
-    for dy, dz in PLANE_STEPS:
+    for dy, dz in PLANE_STEPS[BATCH:]:
         entered(r, ys[dy], zs[dz])
     for other in row_of:
         entered(other, y, z)

time: 47.1 us -> 47.1 us (level)
  no operation moved by 1% of the time
where the time goes in v8:
time: 47.1 us; the launch traced here: 47 us
  Pallas kernels  46.4 us (99%)
  local copies, waits for them, and re-layouts  0.62 us (1%)
    pallas_call x1, Pallas kernels, body(): pl.pallas_call(kernel, out_shape=pltpu.VMEM((2, PTS), F32), in_specs=[pl....  46.4 us

profile of v8, /device:TPU:1, one launch (start us, length us, event | category | flops | bytes accessed | tf_op | source)
XLA Modules:
  0.0 47.0 jit_solution(14750130128946600386)
XLA Ops:
  0.0 46.4 %collocate.1 = f32[2,4096]{1,0:T(2,128)S(1)} custom-call(s32[2,8]{1,0:T(2,128)} %bitcast.5, s32[8]{0:T(128)} %slot_hbm.1, s32[8]{0:T(128)} %tag_hbm.1, s32[1536]{0:T(1024)} %levels_hbm.1, f32[3,1024,128]{2,1,0:T(8,128)} %bitcast.3, f32[1024,128]{1,0:T(8,128)} %exp_hbm.1, bf16[8,128,128]{2,1,0:T(8,128)(2,1)} %block_hbm.1, s32[2,8,256]{2,1,0:T(8,128)} %bitcast.4, ...), custom_call_target="tpu_custom_call" | custom-call | tf_op jit(solution)/shard_map/collocate/pallas_call | solution.py:412
  46.4 0.6 %copy.11 = f32[2,4096]{1,0:T(2,128)} copy(f32[2,4096]{1,0:T(2,128)S(1)} %collocate.1) | data formatting | bytes 65536

commit v9 on v8

--- a/solution.py
+++ b/solution.py
@@ -40,7 +40,6 @@
     (s for s in itertools.product(range(NC), range(NZ)) if any(s)),
     key=lambda s: -(far(s[0], NC) + far(s[1], NZ)),
 )
-CHIP_STEPS = (2, 1, 3, 0)
 ROW_STEPS = ((2, 1), (2, 0), (1, 1), (3, 1), (1, 0), (3, 0), (0, 1))
 
 
@@ -86,8 +85,6 @@
     bricks_ref,
     a_out,
     a_got,
-    h_out,
-    h_got,
     r_out,
     r_got,
     b_out,
@@ -97,8 +94,6 @@
     load_sem,
     a_send,
     a_recv,
-    h_send,
-    h_recv,
     r_send,
     r_recv,
     b_send,
@@ -280,36 +275,19 @@
         mixed = jnp.concatenate([mixed, jnp.zeros((64 - ROWS, 128), F32)], axis=0)
         return jnp.concatenate([whole, jnp.where(half, mixed[:32], mixed[32:])], axis=0)
 
-    halves = []
-    for n, dx in enumerate(CHIP_STEPS):
-        h_out[n] = table(xs[dx] + cores[1])
-        half_copy = pltpu.make_async_remote_copy(
-            src_ref=h_out.at[n],
-            dst_ref=h_got.at[n],
-            send_sem=h_send,
-            recv_sem=h_recv.at[n],
-            device_id=(xs[0] + cores[1], y, z),
-            device_id_type=MESH,
-        )
-        half_copy.start()
-        halves.append(half_copy)
-    for n, dx in enumerate(CHIP_STEPS):
-        r_out[n] = table(xs[dx] + core)
-    for n, dx in enumerate(CHIP_STEPS[:-1]):
-        halves[n].wait_recv()
-        r_out[n] = r_out[n] + h_got[n]
+    for n, other in enumerate(row_of):
+        r_out[n] = table(other)
         pltpu.make_async_remote_copy(
             src_ref=r_out.at[n],
             dst_ref=r_got.at[n],
             send_sem=r_send,
             recv_sem=r_recv,
-            device_id=(xs[dx] + core, y, z),
+            device_id=(other, y, z),
             device_id_type=MESH,
         ).start()
-    halves[-1].wait_recv()
-    total = r_out[NX - 1] + h_got[NX - 1]
-    arrived(r_got, NX - 1, r_recv)
-    for n in range(NX - 1):
+    total = table(r)
+    arrived(r_got, NR - 1, r_recv)
+    for n in range(NR - 1):
         total = total + r_got[n]
     whole, mixed = total[:ROWS], total[ROWS:]
     mixed = jnp.concatenate([mixed, roll(mixed, 64)], axis=0)
@@ -387,8 +365,7 @@
                 value * kept[b][t : t + 1] + added[b][t : t + 1]
             )
     arrived(a_out, PLANE - 1, a_send)
-    arrived(h_out, NX, h_send)
-    arrived(r_out, NX - 1, r_send)
+    arrived(r_out, NR - 1, r_send)
     arrived(b_out, PLANE - 1, b_send)
     arrived(c_got, NR - 1, c_send)
 
@@ -425,18 +402,15 @@
             pltpu.VMEM((128, 128), F32),
             pltpu.VMEM((PLANE - 1, 4, 128), F32),
             pltpu.VMEM((PLANE, 4, 128), F32),
-            pltpu.VMEM((NX, ROWS + 32, 128), F32),
-            pltpu.VMEM((NX, ROWS + 32, 128), F32),
-            pltpu.VMEM((NX, ROWS + 32, 128), F32),
-            pltpu.VMEM((NX - 1, ROWS + 32, 128), F32),
+            pltpu.VMEM((NR - 1, ROWS + 32, 128), F32),
+            pltpu.VMEM((NR - 1, ROWS + 32, 128), F32),
             pltpu.VMEM((PLANE - 1, 1, 128), F32),
             pltpu.VMEM((PLANE, 1, 128), F32),
             pltpu.VMEM((8, 256), F32),
             pltpu.VMEM((NR, 8, 256), F32),
             dma((len(arguments),)),
         ]
-        + [dma, dma, dma, dma((NX,))]
-        + [dma] * 6,
+        + [dma] * 8,
         compiler_params=pltpu.CompilerParams(
             collective_id=0, has_side_effects=True, vmem_limit_bytes=60 * 2**20
         ),

time: 47.1 us -> 46.4 us (0.985)
  Pallas kernels: 46.4 us -> 45.6 us
    pallas_call x1, Pallas kernels: 46.4 us -> 45.6 us  [body(): pl.pallas_call(kernel, out_shape=pltpu.VMEM((2, PTS), F32), in_specs=[pl....]
where the time goes in v9:
time: 46.4 us; the launch traced here: 46.2 us
  Pallas kernels  45.6 us (98%)
  local copies, waits for them, and re-layouts  0.62 us (1%)
    pallas_call x1, Pallas kernels, body(): pl.pallas_call(kernel, out_shape=pltpu.VMEM((2, PTS), F32), in_specs=[pl....  45.6 us

profile of v9, /device:TPU:1, one launch (start us, length us, event | category | flops | bytes accessed | tf_op | source)
XLA Modules:
  0.0 46.2 jit_solution(2890325629273292511)
XLA Ops:
  0.0 45.6 %collocate.1 = f32[2,4096]{1,0:T(2,128)S(1)} custom-call(s32[2,8]{1,0:T(2,128)} %bitcast.5, s32[8]{0:T(128)} %slot_hbm.1, s32[8]{0:T(128)} %tag_hbm.1, s32[1536]{0:T(1024)} %levels_hbm.1, f32[3,1024,128]{2,1,0:T(8,128)} %bitcast.3, f32[1024,128]{1,0:T(8,128)} %exp_hbm.1, bf16[8,128,128]{2,1,0:T(8,128)(2,1)} %block_hbm.1, s32[2,8,256]{2,1,0:T(8,128)} %bitcast.4, ...), custom_call_target="tpu_custom_call" | custom-call | tf_op jit(solution)/shard_map/collocate/pallas_call | solution.py:389
  45.6 0.6 %copy.11 = f32[2,4096]{1,0:T(2,128)} copy(f32[2,4096]{1,0:T(2,128)S(1)} %collocate.1) | data formatting | bytes 65536
